TPU v7x, 32 devices: a whole 2x2x4 slice. The times are simulated.
32 devices in a mesh: phase: 8 (over y, x, core), chan: 4 (over z).
Axes of the slice: x: 2, y: 2, z: 4, core: 2. Of those that a mesh axis runs over, the one named last changes fastest.
Arguments:
- frames: bfloat16 [64, 16, 512], P(None, 'phase', 'chan'), may hold values from -6 to 6
- temporal_taps: float32 [4, 3, 64], replicated, may hold values from -3 to 3
- conv_weights: bfloat16 [4, 64, 27, 2, 64], P(None, None, None, None, 'chan'), may hold values from -0.15625 to 0.15625
- cotangent: bfloat16 [64, 16, 512], P(None, 'phase', 'chan'), may hold values from -16 to 16
Outputs:
- final_frames: bfloat16 [64, 16, 512], P(None, 'phase', 'chan')
- grad_frames: bfloat16 [64, 16, 512], P(None, 'phase', 'chan')
- grad_taps: float32 [4, 3, 64], replicated
- grad_weights: float32 [4, 64, 27, 2, 64], P(None, None, None, None, 'chan')
All inputs are finite; a program needn't handle non-finite values.
Results may differ from a plain program's by a relative error of at most 0.025.
Values may be sent and summed in bfloat16 or wider, within the bound.
A program may use at most 64 MiB of HBM per device.

v0:
```python
import jax
import jax.numpy as jnp
from jax import lax
from jax.sharding import PartitionSpec as P

BLOCKS = 4
SY = 8
SZ = 16


cell_offsets = [
    (kernel_pos // 9 - 1, kernel_pos // 3 % 3 - 1, kernel_pos % 3 - 1) for kernel_pos in range(27)
]


def shifted(block, axis, distance):
    devices = range(lax.axis_size(axis))
    route = [((i - distance) % len(devices), i) for i in devices]
    return lax.ppermute(block, axis, route)


def padded_2(cells, sides, width):
    for axis, dim in sides:
        count = lax.axis_size(axis)
        ends = count - 1
        head = lax.slice_in_dim(cells, 0, width, axis=dim)
        tail = lax.slice_in_dim(cells, cells.shape[dim] - width, cells.shape[dim], axis=dim)
        cells = jnp.concatenate(
            [
                lax.ppermute(tail, axis, [(i, (i + 1) % count) for i in range(ends)]),
                cells,
                lax.ppermute(head, axis, [((i + 1) % count, i) for i in range(ends)]),
            ],
            axis=dim,
        )
    return cells


def within_plane(source, step_y, step_z):
    cell_count = source.shape[-1]
    last_dim = source.ndim - 1
    margin = SZ + 1
    moved = step_y * SZ + step_z
    padded = jnp.pad(source, [(0, 0)] * last_dim + [(margin, margin)])
    window = lax.slice_in_dim(padded, margin + moved, margin + moved + cell_count, axis=last_dim)
    places = jnp.arange(cell_count, dtype=jnp.int32)
    coord_y = places // SZ + step_y
    coord_z = places % SZ + step_z
    inside = (coord_y >= 0) & (coord_y < SY) & (coord_z >= 0) & (coord_z < SZ)
    return jnp.where(inside, window, jnp.zeros_like(window))


def shifted_cells(rimmed, step_x, step_y, step_z):
    planes = rimmed.shape[-2] - 2
    rows = lax.slice_in_dim(rimmed, 1 + step_x, 1 + step_x + planes, axis=rimmed.ndim - 2)
    moved = within_plane(rows, step_y, step_z)
    return moved.reshape(moved.shape[:-2] + (planes * moved.shape[-1],))


def offset_stack(rimmed, first, count, sign):
    picked = cell_offsets[first : first + count]
    return jnp.stack(
        [
            shifted_cells(rimmed, sign * offset[0], sign * offset[1], sign * offset[2])
            for offset in picked
        ],
        axis=1,
    )


def back_block(source, hops):
    if hops == 0:
        return source
    return shifted(source, "phase", hops)


def next_block(source, hops):
    if hops == 0:
        return source
    return shifted(source, "phase", -hops)


def neighbours(source, reach):
    phase_rows = source.shape[1]
    hops, rest = divmod(reach, phase_rows)
    if rest == 0:
        return (back_block(source, hops), next_block(source, hops))
    joined = jnp.concatenate([back_block(source, hops + 1), back_block(source, hops)], axis=1)
    behind = joined[:, phase_rows - rest : 2 * phase_rows - rest]
    joined = jnp.concatenate([next_block(source, hops), next_block(source, hops + 1)], axis=1)
    ahead = joined[:, rest : rest + phase_rows]
    return (behind, ahead)


def per_device(frames, temporal_taps, conv_weights, cotangent):
    chans, phase_rows, cell_count = frames.shape
    plane_cells = SY * SZ
    planes = cell_count // plane_cells
    state = frames
    saved = []
    for block_num in range(BLOCKS):
        reach = 2**block_num
        behind, ahead = neighbours(state, reach)
        tap_rows = temporal_taps[block_num][:, :, None, None]
        mixed = (
            tap_rows[0] * behind.astype(jnp.float32)
            + tap_rows[1] * state.astype(jnp.float32)
            + tap_rows[2] * ahead.astype(jnp.float32)
        ).astype(jnp.bfloat16)
        rimmed = padded_2(mixed.reshape(chans, phase_rows, planes, plane_cells), (("chan", 2),), 1)
        kernel = lax.all_gather(conv_weights[block_num], "chan", axis=3, tiled=True)
        conv_out = jnp.zeros((chans, 2, phase_rows, cell_count), jnp.float32)
        for first in range(0, 27, 9):
            group = offset_stack(rimmed, first, 9, 1)
            conv_out = conv_out + jnp.einsum(
                "ikpv,ikgo->ogpv",
                group,
                kernel[:, first : first + 9],
                preferred_element_type=jnp.float32,
            )
        value_part = conv_out[:, 0]
        gate_sig = jax.nn.sigmoid(conv_out[:, 1])
        saved.append((state, behind, ahead, rimmed, kernel, value_part, gate_sig))
        state = (state.astype(jnp.float32) + value_part * gate_sig).astype(jnp.bfloat16)
    grad_state = cotangent
    weight_grads = [None] * BLOCKS
    tap_grads = [None] * BLOCKS
    for block_num in reversed(range(BLOCKS)):
        reach = 2**block_num
        prior, behind, ahead, rimmed, kernel, value_part, gate_sig = saved[block_num]
        tap_rows = temporal_taps[block_num][:, :, None, None]
        grad_y = grad_state.astype(jnp.float32)
        grad_z = jnp.stack(
            [grad_y * gate_sig, grad_y * value_part * gate_sig * (1.0 - gate_sig)], axis=1
        ).astype(jnp.bfloat16)
        rim_grad = padded_2(
            grad_z.reshape(chans, 2, phase_rows, planes, plane_cells), (("chan", 3),), 1
        )
        grad_mix = jnp.zeros((chans, phase_rows, cell_count), jnp.float32)
        for first in range(0, 27, 3):
            group = offset_stack(rim_grad, first, 3, -1)
            grad_mix = grad_mix + jnp.einsum(
                "okgpv,ikgo->ipv",
                group,
                kernel[:, first : first + 3],
                preferred_element_type=jnp.float32,
            )
        kernel_parts = []
        for first in range(0, 27, 9):
            group = offset_stack(rimmed, first, 9, 1)
            kernel_parts.append(
                jnp.einsum("ikpv,ogpv->ikgo", group, grad_z, preferred_element_type=jnp.float32)
            )
        grad_kernel = jnp.concatenate(kernel_parts, axis=1)
        grad_tap = jnp.stack(
            [
                jnp.sum(grad_mix * behind.astype(jnp.float32), axis=(1, 2)),
                jnp.sum(grad_mix * prior.astype(jnp.float32), axis=(1, 2)),
                jnp.sum(grad_mix * ahead.astype(jnp.float32), axis=(1, 2)),
            ]
        )
        grad_low = grad_mix.astype(jnp.bfloat16)
        back_mix, ahead_mix = neighbours(grad_low, reach)
        grad_state = (
            grad_y
            + tap_rows[0] * ahead_mix.astype(jnp.float32)
            + tap_rows[1] * grad_low.astype(jnp.float32)
            + tap_rows[2] * back_mix.astype(jnp.float32)
        ).astype(jnp.bfloat16)
        kernel_piece = lax.psum_scatter(
            grad_kernel.astype(jnp.bfloat16), "chan", scatter_dimension=3, tiled=True
        )
        grad_kernel = lax.psum(kernel_piece, "phase").astype(jnp.float32)
        weight_grads[block_num] = grad_kernel
        tap_grads[block_num] = grad_tap
    grad_weights = jnp.stack(weight_grads)
    grad_taps = lax.psum(jnp.stack(tap_grads), ("phase", "chan"))
    return (state, grad_state, grad_taps, grad_weights)


def solution(mesh):
    in_specs = (
        P(None, "phase", "chan"),
        P(),
        P(None, None, None, None, "chan"),
        P(None, "phase", "chan"),
    )
    out_specs = (
        P(None, "phase", "chan"),
        P(None, "phase", "chan"),
        P(),
        P(None, None, None, None, "chan"),
    )
    return jax.shard_map(
        per_device, mesh=mesh, in_specs=in_specs, out_specs=out_specs, check_vma=False
    )
```

profile of v0, /device:TPU:0, one launch (start us, length us, event | category | flops | bytes accessed | tf_op | source)
XLA Modules:
  0.0 319.0 jit_solution(5540513160792425908)
XLA Ops:
  8.4 2.9 collective-permute-start.1
  12.9 21.7 %all-gather = bf16[1,64,27,2,64]{1,4,2,3,0:T(8,128)(2,1)S(1)} all-gather(bf16[1,64,27,2,16]{1,4,2,3,0:T(8,128)(2,1)S(1)} %copy.411), channel_id=2, replica_groups=mesh['phase'=8,'chan'=4] {'chan'}, dimensions={4}, use_global_device_ids=true | all-gather | bytes 552960 | tf_op jit(solution)/shard_map/all_gather | solution.py:111
  36.5 4.5 %collective-permute-start.2 = (bf16[64,2,1,128]{3,0,1,2:T(8,128)(2,1)S(1)}, bf16[64,2,1,128]{3,0,1,2:T(8,128)(2,1)S(1)}, u32[]{:S(2)}, u32[]{:S(2)}) collective-permute-start(bf16[64,2,1,128]{3,0,1,2:T(8,128)(2,1)S(1)} %bitcast.1582), channel_id=1, source_target_pairs={{0,1},{1,2},{2,3},{4,5},{5,6},{6,7},{8,9},{9,10},{10,11},{12,13},{... | collective-permute-start | bytes 98312 | tf_op jit(solution)/shard_map/ppermute | solution.py:30
  43.9 2.6 collective-permute-start.5
  46.5 1.6 collective-permute-done.4
  48.2 4.1 %collective-permute-start.6 = (bf16[64,2,1,128]{3,0,1,2:T(8,128)(2,1)S(1)}, bf16[64,2,1,128]{3,0,1,2:T(8,128)(2,1)S(1)}, u32[]{:S(2)}, u32[]{:S(2)}) collective-permute-start(bf16[64,2,1,128]{3,0,1,2:T(8,128)(2,1)S(1)} %bitcast.1561), channel_id=1, source_target_pairs={{0,1},{1,2},{2,3},{4,5},{5,6},{6,7},{8,9},{9,10},{10,11},{12,13},{... | collective-permute-start | bytes 98312 | tf_op jit(solution)/shard_map/ppermute | solution.py:30
  53.7 20.3 %all-gather.1 = bf16[1,64,27,2,64]{1,4,2,3,0:T(8,128)(2,1)S(1)} all-gather(bf16[1,64,27,2,16]{1,4,2,3,0:T(8,128)(2,1)S(1)} %copy.412), channel_id=3, replica_groups=mesh['phase'=8,'chan'=4] {'chan'}, dimensions={4}, use_global_device_ids=true | all-gather | bytes 552960 | tf_op jit(solution)/shard_map/all_gather | solution.py:111
  76.0 2.9 collective-permute-start.9
  78.9 1.9 collective-permute-done.8
  84.2 20.8 %all-gather.2 = bf16[1,64,27,2,64]{1,4,2,3,0:T(8,128)(2,1)S(1)} all-gather(bf16[1,64,27,2,16]{1,4,2,3,0:T(8,128)(2,1)S(1)} %copy.413), channel_id=4, replica_groups=mesh['phase'=8,'chan'=4] {'chan'}, dimensions={4}, use_global_device_ids=true | all-gather | bytes 552960 | tf_op jit(solution)/shard_map/all_gather | solution.py:111
  106.9 1.6 collective-permute-start.12
  108.5 2.3 collective-permute-done.12
  111.0 2.0 collective-permute-start.13
  114.2 19.1 %all-gather.3 = bf16[1,64,27,2,64]{1,4,2,3,0:T(8,128)(2,1)S(1)} all-gather(bf16[1,64,27,2,16]{1,4,2,3,0:T(8,128)(2,1)S(1)} %copy.414), channel_id=5, replica_groups=mesh['phase'=8,'chan'=4] {'chan'}, dimensions={4}, use_global_device_ids=true | all-gather | bytes 552960 | tf_op jit(solution)/shard_map/all_gather | solution.py:111
  137.2 2.3 fusion.229
  139.5 5.2 %collective-permute-start.16 = (bf16[64,2,2,1,128]{4,0,2,1,3:T(8,128)(2,1)}, bf16[64,2,2,1,128]{4,0,2,1,3:T(8,128)(2,1)}, u32[]{:S(2)}, u32[]{:S(2)}) collective-permute-start(bf16[64,2,2,1,128]{4,0,2,1,3:T(8,128)(2,1)} %pad_maximum_fusion.40), channel_id=1, source_target_pairs={{0,1},{1,2},{2,3},{4,5},{5,6},{6,7},{8,9},{9,10},{10,11},{12,13},{... | collective-permute-start | bytes 196616 | tf_op jit(solution)/shard_map/ppermute | solution.py:30
  148.4 1.5 fusion.213
  151.4 1.5 fusion.245
  154.6 1.6 collective-permute-start.17
  156.2 2.3 collective-permute-done.17
  161.7 4.5 %collective-permute-start.19 = (bf16[64,2,2,1,128]{4,0,2,3,1:T(8,128)(2,1)}, bf16[64,2,2,1,128]{4,0,2,3,1:T(8,128)(2,1)S(1)}, u32[]{:S(2)}, u32[]{:S(2)}) collective-permute-start(bf16[64,2,2,1,128]{4,0,2,3,1:T(8,128)(2,1)} %get-tuple-element.100), channel_id=1, source_target_pairs={{0,1},{1,2},{2,3},{4,5},{5,6},{6,7},{8,9},{9,10},{10,11},{12,13},{... | collective-permute-start | bytes 196616 | tf_op jit(solution)/shard_map/ppermute | solution.py:30
  172.1 2.7 collective-permute-start.21
  175.1 1.9 collective-permute-done.21
  177.0 1.7 collective-permute-done.20
  180.4 4.5 %collective-permute-start.23 = (bf16[64,2,2,1,128]{4,0,2,1,3:T(8,128)(2,1)S(1)}, bf16[64,2,2,1,128]{4,0,2,1,3:T(8,128)(2,1)S(1)}, u32[]{:S(2)}, u32[]{:S(2)}) collective-permute-start(bf16[64,2,2,1,128]{4,0,2,1,3:T(8,128)(2,1)S(1)} %pad_maximum_fusion.42), channel_id=1, source_target_pairs={{0,1},{1,2},{2,3},{4,5},{5,6},{6,7},{8,9},{9,10},{10,11},{12,13},{... | collective-permute-start | bytes 196616 | tf_op jit(solution)/shard_map/ppermute | solution.py:30
  190.2 2.6 collective-permute-start.24
  192.9 1.6 collective-permute-done.25
  196.2 4.5 %collective-permute-start.27 = (bf16[64,2,2,1,128]{4,0,2,1,3:T(8,128)(2,1)S(1)}, bf16[64,2,2,1,128]{4,0,2,1,3:T(8,128)(2,1)S(1)}, u32[]{:S(2)}, u32[]{:S(2)}) collective-permute-start(bf16[64,2,2,1,128]{4,0,2,1,3:T(8,128)(2,1)S(1)} %pad_maximum_fusion.43), channel_id=1, source_target_pairs={{0,1},{1,2},{2,3},{4,5},{5,6},{6,7},{8,9},{9,10},{10,11},{12,13},{... | collective-permute-start | bytes 196616 | tf_op jit(solution)/shard_map/ppermute | solution.py:30
  206.1 2.1 collective-permute-start.28
  208.2 41.0 %psum.35 = f32[4,3,64]{2,1,0:T(4,128)S(1)} all-reduce(f32[4,3,64]{2,1,0:T(4,128)S(1)} %pad_maximum_fusion.48), channel_id=1, replica_groups=mesh['phase'=8,'chan'=4] {'phase','chan'}, use_global_device_ids=true, to_apply=%region_11.12 | all-reduce | flops 768 | bytes 6144 | tf_op jit(solution)/shard_map/psum | solution.py:177
  251.6 57.9 %all-reduce.27.cloned.1.call-done = (bf16[1,64,27,2,16]{1,4,2,3,0:T(8,128)(2,1)}, bf16[1,64,27,2,16]{1,4,2,3,0:T(8,128)(2,1)}, bf16[1,64,27,2,16]{1,4,2,3,0:T(8,128)(2,1)}, bf16[1,64,27,2,16]{1,4,2,3,0:T(8,128)(2,1)}) async-done(((bf16[1,64,27,2,16]{1,4,2,3,0:T(8,128)(2,1)}, bf16[1,64,27,2,16]{1,4,2,3,0:T(8,128)(2,1)}, bf16[1,64,27,2,16]{1,4,2,3,0:T(8,128)(2,1)}, bf16[1,64,27,2,16]{1,4,2,3,0:T(8,128)(2,1)}), ...) | async-done | bytes 442384 | tf_op jit(solution)/shard_map/psum | solution.py:173
  309.5 1.6 maximum_convert_fusion
  (369 shorter events, 53.7 us)
Async XLA Ops:
  7.2 242.7 %reduce-scatter.11.cloned.1.call-start = ((), (), s32[]{:S(2)}) async-start(), calls=%async_computation.7 | async-start | bytes 1105920 | tf_op jit(solution)/shard_map/reduce_scatter | solution.py:170
  8.0 26.7 %collective-permute-start = (bf16[64,2,128]{2,0,1:T(8,128)(2,1)S(1)}, bf16[64,2,128]{2,0,1:T(8,128)(2,1)S(1)}, u32[]{:S(2)}, u32[]{:S(2)}) collective-permute-start(bf16[64,2,128]{2,0,1:T(8,128)(2,1)S(1)} %copy.8), channel_id=1, source_target_pairs={{28,0},{0,4},{4,8},{8,12},{12,16},{16,20},{20,24},{24,28},{29,1},{... | collective-permute-start | bytes 98312 | tf_op jit(solution)/shard_map/ppermute | solution.py:19
  8.4 26.3 %collective-permute-start.1 = (bf16[64,2,128]{2,0,1:T(8,128)(2,1)S(1)}, bf16[64,2,128]{2,0,1:T(8,128)(2,1)S(1)}, u32[]{:S(2)}, u32[]{:S(2)}) collective-permute-start(bf16[64,2,128]{2,0,1:T(8,128)(2,1)S(1)} %copy.8), channel_id=1, source_target_pairs={{4,0},{8,4},{12,8},{16,12},{20,16},{24,20},{28,24},{0,28},{5,1},{9... | collective-permute-start | bytes 98312 | tf_op jit(solution)/shard_map/ppermute | solution.py:19
  35.2 5.9 %collective-permute-start.3 = (bf16[64,2,1,128]{3,0,1,2:T(8,128)(2,1)S(1)}, bf16[64,2,1,128]{3,0,1,2:T(8,128)(2,1)S(1)}, u32[]{:S(2)}, u32[]{:S(2)}) collective-permute-start(bf16[64,2,1,128]{3,0,1,2:T(8,128)(2,1)S(1)} %bitcast.1581), channel_id=1, source_target_pairs={{1,0},{2,1},{3,2},{5,4},{6,5},{7,6},{9,8},{10,9},{11,10},{13,12},{... | collective-permute-start | bytes 98312 | tf_op jit(solution)/shard_map/ppermute | solution.py:32
  36.5 6.2 %collective-permute-start.2 = (bf16[64,2,1,128]{3,0,1,2:T(8,128)(2,1)S(1)}, bf16[64,2,1,128]{3,0,1,2:T(8,128)(2,1)S(1)}, u32[]{:S(2)}, u32[]{:S(2)}) collective-permute-start(bf16[64,2,1,128]{3,0,1,2:T(8,128)(2,1)S(1)} %bitcast.1582), channel_id=1, source_target_pairs={{0,1},{1,2},{2,3},{4,5},{5,6},{6,7},{8,9},{9,10},{10,11},{12,13},{... | collective-permute-start | bytes 98312 | tf_op jit(solution)/shard_map/ppermute | solution.py:30
  43.8 4.3 %collective-permute-start.4 = (bf16[64,2,128]{2,0,1:T(8,128)(2,1)S(1)}, bf16[64,2,128]{2,0,1:T(8,128)(2,1)S(1)}, u32[]{:S(2)}, u32[]{:S(2)}) collective-permute-start(bf16[64,2,128]{2,0,1:T(8,128)(2,1)S(1)} %fusion.161), channel_id=1, source_target_pairs={{28,0},{0,4},{4,8},{8,12},{12,16},{16,20},{20,24},{24,28},{29,1},{... | collective-permute-start | bytes 98312 | tf_op jit(solution)/shard_map/ppermute | solution.py:19
  43.9 4.2 %collective-permute-start.5 = (bf16[64,2,128]{2,0,1:T(8,128)(2,1)S(1)}, bf16[64,2,128]{2,0,1:T(8,128)(2,1)S(1)}, u32[]{:S(2)}, u32[]{:S(2)}) collective-permute-start(bf16[64,2,128]{2,0,1:T(8,128)(2,1)S(1)} %fusion.161), channel_id=1, source_target_pairs={{4,0},{8,4},{12,8},{16,12},{20,16},{24,20},{28,24},{0,28},{5,1},{9... | collective-permute-start | bytes 98312 | tf_op jit(solution)/shard_map/ppermute | solution.py:19
  48.2 25.8 %collective-permute-start.6 = (bf16[64,2,1,128]{3,0,1,2:T(8,128)(2,1)S(1)}, bf16[64,2,1,128]{3,0,1,2:T(8,128)(2,1)S(1)}, u32[]{:S(2)}, u32[]{:S(2)}) collective-permute-start(bf16[64,2,1,128]{3,0,1,2:T(8,128)(2,1)S(1)} %bitcast.1561), channel_id=1, source_target_pairs={{0,1},{1,2},{2,3},{4,5},{5,6},{6,7},{8,9},{9,10},{10,11},{12,13},{... | collective-permute-start | bytes 98312 | tf_op jit(solution)/shard_map/ppermute | solution.py:30
  52.4 21.6 %collective-permute-start.7 = (bf16[64,2,1,128]{3,0,1,2:T(8,128)(2,1)S(1)}, bf16[64,2,1,128]{3,0,1,2:T(8,128)(2,1)S(1)}, u32[]{:S(2)}, u32[]{:S(2)}) collective-permute-start(bf16[64,2,1,128]{3,0,1,2:T(8,128)(2,1)S(1)} %bitcast.1562), channel_id=1, source_target_pairs={{1,0},{2,1},{3,2},{5,4},{6,5},{7,6},{9,8},{10,9},{11,10},{13,12},{... | collective-permute-start | bytes 98312 | tf_op jit(solution)/shard_map/ppermute | solution.py:32
  75.9 4.9 %collective-permute-start.8 = (bf16[64,2,128]{2,0,1:T(8,128)(2,1)S(1)}, bf16[64,2,128]{2,0,1:T(8,128)(2,1)S(1)}, u32[]{:S(2)}, u32[]{:S(2)}) collective-permute-start(bf16[64,2,128]{2,0,1:T(8,128)(2,1)S(1)} %fusion.163), channel_id=1, source_target_pairs={{24,0},{28,4},{0,8},{4,12},{8,16},{12,20},{16,24},{20,28},{25,1},{... | collective-permute-start | bytes 98312 | tf_op jit(solution)/shard_map/ppermute | solution.py:19
  76.0 5.5 %collective-permute-start.9 = (bf16[64,2,128]{2,0,1:T(8,128)(2,1)S(1)}, bf16[64,2,128]{2,0,1:T(8,128)(2,1)S(1)}, u32[]{:S(2)}, u32[]{:S(2)}) collective-permute-start(bf16[64,2,128]{2,0,1:T(8,128)(2,1)S(1)} %fusion.163), channel_id=1, source_target_pairs={{8,0},{12,4},{16,8},{20,12},{24,16},{28,20},{0,24},{4,28},{9,1},{1... | collective-permute-start | bytes 98312 | tf_op jit(solution)/shard_map/ppermute | solution.py:19
  81.6 23.4 %collective-permute-start.10 = (bf16[64,2,1,128]{3,0,1,2:T(8,128)(2,1)S(1)}, bf16[64,2,1,128]{3,0,1,2:T(8,128)(2,1)S(1)}, u32[]{:S(2)}, u32[]{:S(2)}) collective-permute-start(bf16[64,2,1,128]{3,0,1,2:T(8,128)(2,1)S(1)} %bitcast.1571), channel_id=1, source_target_pairs={{0,1},{1,2},{2,3},{4,5},{5,6},{6,7},{8,9},{9,10},{10,11},{12,13},{... | collective-permute-start | bytes 98312 | tf_op jit(solution)/shard_map/ppermute | solution.py:30
  82.9 22.1 %collective-permute-start.11 = (bf16[64,2,1,128]{3,0,1,2:T(8,128)(2,1)S(1)}, bf16[64,2,1,128]{3,0,1,2:T(8,128)(2,1)S(1)}, u32[]{:S(2)}, u32[]{:S(2)}) collective-permute-start(bf16[64,2,1,128]{3,0,1,2:T(8,128)(2,1)S(1)} %bitcast.1572), channel_id=1, source_target_pairs={{1,0},{2,1},{3,2},{5,4},{6,5},{7,6},{9,8},{10,9},{11,10},{13,12},{... | collective-permute-start | bytes 98312 | tf_op jit(solution)/shard_map/ppermute | solution.py:32
  111.0 22.4 %collective-permute-start.13 = (bf16[64,2,1,128]{3,0,1,2:T(8,128)(2,1)S(1)}, bf16[64,2,1,128]{3,0,1,2:T(8,128)(2,1)S(1)}, u32[]{:S(2)}, u32[]{:S(2)}) collective-permute-start(bf16[64,2,1,128]{3,0,1,2:T(8,128)(2,1)S(1)} %bitcast.1551), channel_id=1, source_target_pairs={{0,1},{1,2},{2,3},{4,5},{5,6},{6,7},{8,9},{9,10},{10,11},{12,13},{... | collective-permute-start | bytes 98312 | tf_op jit(solution)/shard_map/ppermute | solution.py:30
  112.9 20.5 %collective-permute-start.14 = (bf16[64,2,1,128]{3,0,1,2:T(8,128)(2,1)S(1)}, bf16[64,2,1,128]{3,0,1,2:T(8,128)(2,1)S(1)}, u32[]{:S(2)}, u32[]{:S(2)}) collective-permute-start(bf16[64,2,1,128]{3,0,1,2:T(8,128)(2,1)S(1)} %bitcast.1552), channel_id=1, source_target_pairs={{1,0},{2,1},{3,2},{5,4},{6,5},{7,6},{9,8},{10,9},{11,10},{13,12},{... | collective-permute-start | bytes 98312 | tf_op jit(solution)/shard_map/ppermute | solution.py:32
  135.9 12.5 %collective-permute-start.15 = (bf16[64,2,2,1,128]{4,0,2,1,3:T(8,128)(2,1)}, bf16[64,2,2,1,128]{4,0,2,1,3:T(8,128)(2,1)}, u32[]{:S(2)}, u32[]{:S(2)}) collective-permute-start(bf16[64,2,2,1,128]{4,0,2,1,3:T(8,128)(2,1)} %pad_maximum_fusion.40), channel_id=1, source_target_pairs={{1,0},{2,1},{3,2},{5,4},{6,5},{7,6},{9,8},{10,9},{11,10},{13,12},{... | collective-permute-start | bytes 196616 | tf_op jit(solution)/shard_map/ppermute | solution.py:32
  139.5 11.9 %collective-permute-start.16 = (bf16[64,2,2,1,128]{4,0,2,1,3:T(8,128)(2,1)}, bf16[64,2,2,1,128]{4,0,2,1,3:T(8,128)(2,1)}, u32[]{:S(2)}, u32[]{:S(2)}) collective-permute-start(bf16[64,2,2,1,128]{4,0,2,1,3:T(8,128)(2,1)} %pad_maximum_fusion.40), channel_id=1, source_target_pairs={{0,1},{1,2},{2,3},{4,5},{5,6},{6,7},{8,9},{9,10},{10,11},{12,13},{... | collective-permute-start | bytes 196616 | tf_op jit(solution)/shard_map/ppermute | solution.py:30
  147.3 102.5 %reduce-scatter.9.cloned.1.call-start = ((), (), s32[]{:S(2)}) async-start(), calls=%async_computation.6 | async-start | bytes 1105920 | tf_op jit(solution)/shard_map/reduce_scatter | solution.py:170
  159.4 10.1 %collective-permute-start.18 = (bf16[64,2,2,1,128]{4,0,2,1,3:T(8,128)(2,1)S(1)}, bf16[64,2,2,1,128]{4,0,2,1,3:T(8,128)(2,1)S(1)}, u32[]{:S(2)}, u32[]{:S(2)}) collective-permute-start(bf16[64,2,2,1,128]{4,0,2,1,3:T(8,128)(2,1)S(1)} %get-tuple-element.101), channel_id=1, source_target_pairs={{1,0},{2,1},{3,2},{5,4},{6,5},{7,6},{9,8},{10,9},{11,10},{13,12},{... | collective-permute-start | bytes 196616 | tf_op jit(solution)/shard_map/ppermute | solution.py:32
  161.7 7.5 %collective-permute-start.19 = (bf16[64,2,2,1,128]{4,0,2,3,1:T(8,128)(2,1)}, bf16[64,2,2,1,128]{4,0,2,3,1:T(8,128)(2,1)S(1)}, u32[]{:S(2)}, u32[]{:S(2)}) collective-permute-start(bf16[64,2,2,1,128]{4,0,2,3,1:T(8,128)(2,1)} %get-tuple-element.100), channel_id=1, source_target_pairs={{0,1},{1,2},{2,3},{4,5},{5,6},{6,7},{8,9},{9,10},{10,11},{12,13},{... | collective-permute-start | bytes 196616 | tf_op jit(solution)/shard_map/ppermute | solution.py:30
  169.0 80.8 %reduce-scatter.7.cloned.1.call-start = ((), (), s32[]{:S(2)}) async-start(), calls=%async_computation.5 | async-start | bytes 1105920 | tf_op jit(solution)/shard_map/reduce_scatter | solution.py:170
  172.1 4.9 %collective-permute-start.21 = (bf16[64,2,128]{2,0,1:T(8,128)(2,1)S(1)}, bf16[64,2,128]{2,0,1:T(8,128)(2,1)S(1)}, u32[]{:S(2)}, u32[]{:S(2)}) collective-permute-start(bf16[64,2,128]{2,0,1:T(8,128)(2,1)S(1)} %get-tuple-element.38), channel_id=1, source_target_pairs={{24,0},{28,4},{0,8},{4,12},{8,16},{12,20},{16,24},{20,28},{25,1},{... | collective-permute-start | bytes 98312 | tf_op jit(solution)/shard_map/ppermute | solution.py:19
  178.8 8.7 %collective-permute-start.22 = (bf16[64,2,2,1,128]{4,0,2,1,3:T(8,128)(2,1)S(1)}, bf16[64,2,2,1,128]{4,0,2,1,3:T(8,128)(2,1)S(1)}, u32[]{:S(2)}, u32[]{:S(2)}) collective-permute-start(bf16[64,2,2,1,128]{4,0,2,1,3:T(8,128)(2,1)S(1)} %pad_maximum_fusion.42), channel_id=1, source_target_pairs={{1,0},{2,1},{3,2},{5,4},{6,5},{7,6},{9,8},{10,9},{11,10},{13,12},{... | collective-permute-start | bytes 196616 | tf_op jit(solution)/shard_map/ppermute | solution.py:32
  180.4 8.7 %collective-permute-start.23 = (bf16[64,2,2,1,128]{4,0,2,1,3:T(8,128)(2,1)S(1)}, bf16[64,2,2,1,128]{4,0,2,1,3:T(8,128)(2,1)S(1)}, u32[]{:S(2)}, u32[]{:S(2)}) collective-permute-start(bf16[64,2,2,1,128]{4,0,2,1,3:T(8,128)(2,1)S(1)} %pad_maximum_fusion.42), channel_id=1, source_target_pairs={{0,1},{1,2},{2,3},{4,5},{5,6},{6,7},{8,9},{9,10},{10,11},{12,13},{... | collective-permute-start | bytes 196616 | tf_op jit(solution)/shard_map/ppermute | solution.py:30
  187.0 63.7 %reduce-scatter.5.cloned.1.call-start = ((), (), s32[]{:S(2)}) async-start(), calls=%async_computation.4 | async-start | bytes 1105920 | tf_op jit(solution)/shard_map/reduce_scatter | solution.py:170
  190.2 4.3 %collective-permute-start.25 = (bf16[64,2,128]{2,0,1:T(8,128)(2,1)S(1)}, bf16[64,2,128]{2,0,1:T(8,128)(2,1)S(1)}, u32[]{:S(2)}, u32[]{:S(2)}) collective-permute-start(bf16[64,2,128]{2,0,1:T(8,128)(2,1)S(1)} %get-tuple-element.37), channel_id=1, source_target_pairs={{28,0},{0,4},{4,8},{8,12},{12,16},{16,20},{20,24},{24,28},{29,1},{... | collective-permute-start | bytes 98312 | tf_op jit(solution)/shard_map/ppermute | solution.py:19
  190.2 4.2 %collective-permute-start.24 = (bf16[64,2,128]{2,0,1:T(8,128)(2,1)S(1)}, bf16[64,2,128]{2,0,1:T(8,128)(2,1)S(1)}, u32[]{:S(2)}, u32[]{:S(2)}) collective-permute-start(bf16[64,2,128]{2,0,1:T(8,128)(2,1)S(1)} %get-tuple-element.37), channel_id=1, source_target_pairs={{4,0},{8,4},{12,8},{16,12},{20,16},{24,20},{28,24},{0,28},{5,1},{9... | collective-permute-start | bytes 98312 | tf_op jit(solution)/shard_map/ppermute | solution.py:19
  194.6 8.2 %collective-permute-start.26 = (bf16[64,2,2,1,128]{4,0,2,1,3:T(8,128)(2,1)S(1)}, bf16[64,2,2,1,128]{4,0,2,1,3:T(8,128)(2,1)S(1)}, u32[]{:S(2)}, u32[]{:S(2)}) collective-permute-start(bf16[64,2,2,1,128]{4,0,2,1,3:T(8,128)(2,1)S(1)} %pad_maximum_fusion.43), channel_id=1, source_target_pairs={{1,0},{2,1},{3,2},{5,4},{6,5},{7,6},{9,8},{10,9},{11,10},{13,12},{... | collective-permute-start | bytes 196616 | tf_op jit(solution)/shard_map/ppermute | solution.py:32
  196.2 8.3 %collective-permute-start.27 = (bf16[64,2,2,1,128]{4,0,2,1,3:T(8,128)(2,1)S(1)}, bf16[64,2,2,1,128]{4,0,2,1,3:T(8,128)(2,1)S(1)}, u32[]{:S(2)}, u32[]{:S(2)}) collective-permute-start(bf16[64,2,2,1,128]{4,0,2,1,3:T(8,128)(2,1)S(1)} %pad_maximum_fusion.43), channel_id=1, source_target_pairs={{0,1},{1,2},{2,3},{4,5},{5,6},{6,7},{8,9},{9,10},{10,11},{12,13},{... | collective-permute-start | bytes 196616 | tf_op jit(solution)/shard_map/ppermute | solution.py:30
  202.8 106.7 %all-reduce.27.cloned.1.call-start = ((), (), s32[]{:S(2)}) async-start(), calls=%async_computation.8 | async-start | bytes 1769472 | tf_op jit(solution)/shard_map/psum | solution.py:173
  205.5 45.3 %collective-permute-start.29 = (bf16[64,2,128]{2,0,1:T(8,128)(2,1)S(1)}, bf16[64,2,128]{2,0,1:T(8,128)(2,1)S(1)}, u32[]{:S(2)}, u32[]{:S(2)}) collective-permute-start(bf16[64,2,128]{2,0,1:T(8,128)(2,1)S(1)} %get-tuple-element.36), channel_id=1, source_target_pairs={{28,0},{0,4},{4,8},{8,12},{12,16},{16,20},{20,24},{24,28},{29,1},{... | collective-permute-start | bytes 98312 | tf_op jit(solution)/shard_map/ppermute | solution.py:19
  206.1 44.7 %collective-permute-start.28 = (bf16[64,2,128]{2,0,1:T(8,128)(2,1)S(1)}, bf16[64,2,128]{2,0,1:T(8,128)(2,1)S(1)}, u32[]{:S(2)}, u32[]{:S(2)}) collective-permute-start(bf16[64,2,128]{2,0,1:T(8,128)(2,1)S(1)} %get-tuple-element.36), channel_id=1, source_target_pairs={{4,0},{8,4},{12,8},{16,12},{20,16},{24,20},{28,24},{0,28},{5,1},{9... | collective-permute-start | bytes 98312 | tf_op jit(solution)/shard_map/ppermute | solution.py:19
  (76 other events, 1037.4 us)
Sparse Core Ops, SparseCore 0:
  147.4 24.2 reduce-scatter.10
  174.1 23.9 reduce-scatter.8
  200.9 23.7 reduce-scatter.6
  226.9 23.8 reduce-scatter.4
  254.1 55.2 all-reduce.26
where the time goes:
time: 320 us; the launch traced here: 319 us
  blocking collectives  123 us (38%)
  waiting for transfers between devices  73.4 us (23%)
  starting transfers between devices  62.1 us (19%)
  other arithmetic  23.7 us (7%)
  between operations  15.7 us (5%)
  matrix products  14.8 us (5%)
  local copies, waits for them, and re-layouts  6.33 us (2%)
    all_gather x4, blocking collectives, per_device(): kernel = lax.all_gather(conv_weights[block_num], 'chan', axis=3, tiled=True)  81.9 us
    psum x1, waiting for transfers between devices, per_device(): grad_kernel = lax.psum(kernel_piece, 'phase').astype(jnp.float32)  57.9 us
    psum x1, blocking collectives, per_device(): grad_taps = lax.psum(jnp.stack(tap_grads), ('phase', 'chan'))  41 us
    ppermute x8, starting transfers between devices, padded_2(): lax.ppermute(tail, axis, [(i, (i + 1) % count) for i in range(ends)])  30.8 us
    ppermute x14, starting transfers between devices, shifted(): return lax.ppermute(block, axis, route)  20.7 us
    ppermute x14, waiting for transfers between devices, shifted(): return lax.ppermute(block, axis, route)  14 us
    another operation x22, other arithmetic, offset_stack(): jnp.stack([shifted_cells(rimmed, sign * offset[0], sign * offset[1], sign...  10.7 us
    ppermute x8, starting transfers between devices, padded_2(): lax.ppermute(head, axis, [((i + 1) % count, i) for i in range(ends)])  10.3 us
  transfers between devices with their start and end apart: 35, of which 11 were waited for; matrix products, arithmetic and copies ran while one was open for 10% of the time, Pallas kernels for 0%

commit v1 on v0

--- a/solution.py
+++ b/solution.py
@@ -1,6 +1,10 @@
+import functools
+
 import jax
 import jax.numpy as jnp
 from jax import lax
+from jax.experimental import pallas as pl
+from jax.experimental.pallas import tpu as pltpu
 from jax.sharding import PartitionSpec as P
 
 BLOCKS = 4
@@ -178,6 +182,440 @@
     return (state, grad_state, grad_taps, grad_weights)
 
 
+class Copies:
+    def __init__(self, send_sems, recv_sems):
+        self.send_sems = send_sems
+        self.recv_sems = recv_sems
+        self.started = []
+
+    def send(self, src, dst, target):
+        number = len(self.started)
+        copy = pltpu.make_async_remote_copy(
+            src_ref=src,
+            dst_ref=dst,
+            send_sem=self.send_sems.at[number],
+            recv_sem=self.recv_sems.at[number],
+            device_id=target,
+            device_id_type=pl.DeviceIdType.MESH,
+        )
+        copy.start()
+        self.started.append(copy)
+        return copy
+
+
+def copy_count(phase_n, chan_n, blocks):
+    return (
+        4 * (chan_n - 1)
+        + blocks * (2 + (chan_n - 1))
+        + blocks * ((chan_n - 1) + 2 + 2 * (phase_n - 1))
+        + (phase_n - 1)
+        + (chan_n - 1)
+    )
+
+
+def plane_shift(array, step, phase_rows):
+    if step == 0:
+        return array
+    width = array.shape[1] // phase_rows
+    cells = SY * SZ
+    blank = jnp.zeros((array.shape[0], cells), array.dtype)
+    pieces = []
+    for row in range(phase_rows):
+        base = row * width
+        if step < 0:
+            pieces += [blank, array[:, base : base + width - cells]]
+        else:
+            pieces += [array[:, base + cells : base + width], blank]
+    return jnp.concatenate(pieces, axis=1)
+
+
+def fused_kernel(
+    dims,
+    frames,
+    cotangent,
+    taps,
+    w_fwd,
+    w_bwd,
+    final_out,
+    grad_out,
+    gw_out,
+    taps_out,
+    fr_x,
+    cot_x,
+    state,
+    behind_b,
+    ahead_b,
+    mixed,
+    stack,
+    value,
+    gate,
+    gz_stack,
+    gm_send,
+    gm_full,
+    gm_recv,
+    gl,
+    gl_back,
+    gl_ahead,
+    gw_send,
+    gw_recv,
+    tap_send,
+    tap_recv,
+    final_send,
+    grad_send,
+    send_sems,
+    recv_sems,
+):
+    phase_n, chan_n, phase_rows, own, whole, chunk = dims
+    chans = own * chan_n
+    width = phase_rows * whole
+    local = whole // chan_n
+    cells = SY * SZ
+    p = lax.axis_index("phase")
+    z = lax.axis_index("chan")
+    copies = Copies(send_sems, recv_sems)
+    f32, b16 = jnp.float32, jnp.bfloat16
+
+    def at_phase(hop):
+        return {"phase": lax.rem(p + (hop % phase_n), phase_n), "chan": z}
+
+    def at_chan(hop):
+        return {"phase": p, "chan": lax.rem(z + (hop % chan_n), chan_n)}
+
+    def rows_of(index):
+        return pl.ds(pl.multiple_of(index * own, own), own)
+
+    barrier = pltpu.get_barrier_semaphore()
+    for hop in range(1, phase_n):
+        pl.semaphore_signal(
+            barrier, inc=1, device_id=at_phase(hop), device_id_type=pl.DeviceIdType.MESH
+        )
+    for hop in range(1, chan_n):
+        pl.semaphore_signal(
+            barrier, inc=1, device_id=at_chan(hop), device_id_type=pl.DeviceIdType.MESH
+        )
+    pl.semaphore_wait(barrier, phase_n + chan_n - 2)
+
+    lane = lax.broadcasted_iota(jnp.int32, (1, width), 1)
+    coord_z = lax.rem(lane, SZ)
+    coord_y = lax.rem(lane // SZ, SY)
+    steps = [(k // 3 - 1, k % 3 - 1) for k in range(9)]
+    masks = {}
+    for step_y, step_z in steps:
+        y, w = coord_y + step_y, coord_z + step_z
+        masks[step_y, step_z] = (
+            ((y >= 0) & (y < SY) & (w >= 0) & (w < SZ)).astype(f32)
+        )
+
+    def cell_shifts(array, sign):
+        for step_y, step_z in steps:
+            step_y, step_z = sign * step_y, sign * step_z
+            moved = step_y * SZ + step_z
+            if moved == 0:
+                yield array.astype(b16)
+            else:
+                rolled = pltpu.roll(array, (-moved) % width, axis=1)
+                yield (rolled * masks[step_y, step_z]).astype(b16)
+
+    def spread_rows(source, target):
+        got = []
+        for hop in range(1, chan_n):
+            there = at_chan(hop)
+            got.append(copies.send(source.at[rows_of(there["chan"])], target.at[z], there))
+        target[z] = source[rows_of(z), :]
+        return got
+
+    def join_planes(parts):
+        pieces = []
+        for row in range(phase_rows):
+            for index in range(chan_n):
+                pieces.append(parts[index, :, row * local : (row + 1) * local])
+        return jnp.concatenate(pieces, axis=1)
+
+    def spread_planes(array, stage, target):
+        for index in range(chan_n):
+            stage[index] = jnp.concatenate(
+                [
+                    array[:, row * whole + index * local : row * whole + (index + 1) * local]
+                    for row in range(phase_rows)
+                ],
+                axis=1,
+            )
+        got = []
+        for hop in range(1, chan_n):
+            there = at_chan(hop)
+            got.append(copies.send(stage.at[there["chan"]], target.at[z], there))
+        target[z] = stage[z]
+        return got
+
+    def start_neighbours(source, back, ahead, reach):
+        hops, rest = divmod(reach, phase_rows)
+        if rest:
+            edge = rest * whole
+            got = [
+                copies.send(source.at[:, width - edge :], back.at[:, :edge], at_phase(1)),
+                copies.send(source.at[:, :edge], ahead.at[:, width - edge :], at_phase(-1)),
+            ]
+            back[:, edge:] = source[:, : width - edge]
+            ahead[:, : width - edge] = source[:, edge:]
+            return got
+        if (2 * hops) % phase_n == 0:
+            return [copies.send(source, back, at_phase(hops))]
+        return [
+            copies.send(source, back, at_phase(hops)),
+            copies.send(source, ahead, at_phase(-hops)),
+        ]
+
+    def read_neighbours(back, ahead, got):
+        for copy in got:
+            copy.wait_recv()
+        back_values = back[...].astype(f32)
+        if len(got) == 1:
+            return back_values, back_values
+        return back_values, ahead[...].astype(f32)
+
+    def wait_all(got):
+        for copy in got:
+            copy.wait_recv()
+
+    got_frames = spread_rows(frames, fr_x)
+    got_cotangent = spread_rows(cotangent, cot_x)
+    own_taps = taps[rows_of(z), :]
+
+    def tap(block, index):
+        number = 3 * block + index
+        return own_taps[:, number : number + 1]
+
+    wait_all(got_frames)
+    state[0] = join_planes(fr_x)
+
+    single = []
+    for block in range(BLOCKS):
+        reach = 2**block
+        got = start_neighbours(state.at[block], behind_b.at[block], ahead_b.at[block], reach)
+        single.append(len(got) == 1)
+        here = state[block].astype(f32)
+        back, ahead = read_neighbours(behind_b.at[block], ahead_b.at[block], got)
+        mix = tap(block, 0) * back + tap(block, 1) * here + tap(block, 2) * ahead
+        mixed[block, rows_of(z), :] = mix.astype(b16)
+        got = []
+        for hop in range(1, chan_n):
+            part = mixed.at[block, rows_of(z), :]
+            got.append(copies.send(part, part, at_chan(hop)))
+        wait_all(got)
+        full = mixed[block].astype(f32)
+        for number, moved in enumerate(cell_shifts(full, 1)):
+            stack[block, number * chans : (number + 1) * chans, :] = moved
+        parts = jnp.dot(w_fwd[block], stack[block], preferred_element_type=f32)
+        rows = 2 * own
+        conv = (
+            parts[rows : 2 * rows]
+            + plane_shift(parts[:rows], -1, phase_rows)
+            + plane_shift(parts[2 * rows :], 1, phase_rows)
+        )
+        sig = jax.nn.sigmoid(conv[own:])
+        value[block] = conv[:own]
+        gate[block] = sig
+        state[block + 1] = (here + conv[:own] * sig).astype(b16)
+
+    got_final = spread_planes(state[BLOCKS], final_send, final_out)
+
+    wait_all(got_cotangent)
+    grad = join_planes(cot_x).astype(f32)
+    tap_lane = lax.broadcasted_iota(jnp.int32, tap_send.shape, 1)
+    tap_sums = jnp.zeros(tap_send.shape, f32)
+    got_final_grads = []
+
+    def reduce_kernel(block, got):
+        wait_all(got)
+        total = gw_send[block, rows_chunk(p), :].astype(f32)
+        for hop in range(1, phase_n):
+            source = lax.rem(p + hop, phase_n)
+            total = total + gw_recv[block, source].astype(f32)
+        gw_out[block, p] = total.astype(b16)
+        for hop in range(1, phase_n):
+            part = gw_out.at[block, p]
+            got_final_grads.append(copies.send(part, part, at_phase(hop)))
+
+    def rows_chunk(index):
+        return pl.ds(pl.multiple_of(index * chunk, chunk), chunk)
+
+    waiting = None
+    for block in reversed(range(BLOCKS)):
+        reach = 2**block
+        sig, val = gate[block], value[block]
+        gz = jnp.concatenate([grad * sig, grad * val * sig * (1.0 - sig)], axis=0)
+        for number, moved in enumerate(cell_shifts(gz.astype(b16).astype(f32), -1)):
+            gz_stack[number * 2 * own : (number + 1) * 2 * own, :] = moved
+        parts = jnp.dot(w_bwd[block], gz_stack[...], preferred_element_type=f32)
+        gm = (
+            parts[chans : 2 * chans]
+            + plane_shift(parts[:chans], 1, phase_rows)
+            + plane_shift(parts[2 * chans :], -1, phase_rows)
+        )
+        gm_send[block] = gm.astype(b16)
+        gm_full[...] = gm
+        got = []
+        for hop in range(1, chan_n):
+            there = at_chan(hop)
+            got.append(
+                copies.send(
+                    gm_send.at[block, rows_of(there["chan"]), :], gm_recv.at[block, z], there
+                )
+            )
+        low = gz.astype(b16)
+        sides = jnp.concatenate(
+            [plane_shift(low, 1, phase_rows), low, plane_shift(low, -1, phase_rows)], axis=0
+        )
+        products = lax.dot_general(
+            stack[block], sides, (((1,), (1,)), ((), ())), preferred_element_type=f32
+        )
+        gw_send[block, : products.shape[0], :] = products.astype(b16)
+        extra = gw_send.shape[1] - products.shape[0]
+        if extra:
+            gw_send[block, products.shape[0] :, :] = jnp.zeros((extra, products.shape[1]), b16)
+        kernel_got = []
+        for hop in range(1, phase_n):
+            there = at_phase(hop)
+            kernel_got.append(
+                copies.send(
+                    gw_send.at[block, rows_chunk(there["phase"]), :], gw_recv.at[block, p], there
+                )
+            )
+        wait_all(got)
+        mix_grad = gm_full[rows_of(z), :]
+        for hop in range(1, chan_n):
+            mix_grad = mix_grad + gm_recv[block, lax.rem(z + hop, chan_n)].astype(f32)
+        gl[block] = mix_grad.astype(b16)
+        got = start_neighbours(gl.at[block], gl_back.at[block], gl_ahead.at[block], reach)
+        ahead_state = behind_b if single[block] else ahead_b
+        for index, factor in enumerate((behind_b, state, ahead_state)):
+            total = jnp.sum(mix_grad * factor[block].astype(f32), axis=1, keepdims=True)
+            tap_sums = jnp.where(tap_lane == 3 * block + index, total, tap_sums)
+        if waiting is not None:
+            reduce_kernel(*waiting)
+        waiting = (block, kernel_got)
+        low = gl[block].astype(f32)
+        back, ahead = read_neighbours(gl_back.at[block], gl_ahead.at[block], got)
+        moved = grad + tap(block, 0) * ahead + tap(block, 1) * low + tap(block, 2) * back
+        rounded = moved.astype(b16)
+        grad = rounded.astype(f32)
+        if block == 0:
+            tap_send[...] = tap_sums
+            tap_got = []
+            for hop in range(1, phase_n):
+                tap_got.append(copies.send(tap_send, tap_recv.at[p], at_phase(hop)))
+            got_grad = spread_planes(rounded, grad_send, grad_out)
+
+    reduce_kernel(*waiting)
+    wait_all(tap_got)
+    tap_recv[p] = tap_send[...]
+    total = tap_recv[0]
+    for index in range(1, phase_n):
+        total = total + tap_recv[index]
+    taps_out[z] = total
+    got_taps = []
+    for hop in range(1, chan_n):
+        part = taps_out.at[z]
+        got_taps.append(copies.send(part, part, at_chan(hop)))
+    wait_all(got_final)
+    wait_all(got_grad)
+    wait_all(got_taps)
+    wait_all(got_final_grads)
+    for copy in copies.started:
+        copy.wait_send()
+
+
+def fused(frames, temporal_taps, conv_weights, cotangent):
+    chans, phase_rows, local = frames.shape
+    phase_n, chan_n = lax.axis_size("phase"), lax.axis_size("chan")
+    own = chans // chan_n
+    whole = local * chan_n
+    width = phase_rows * whole
+    flat = phase_rows * local
+    stack_rows = 9 * chans
+    chunk = -(-stack_rows // (16 * phase_n)) * 16
+    b16, f32 = jnp.bfloat16, jnp.float32
+    split = conv_weights.reshape(BLOCKS, chans, 3, 9, 2, own)
+    w_fwd = jnp.transpose(split, (0, 2, 4, 5, 3, 1)).reshape(BLOCKS, 6 * own, 9 * chans)
+    w_bwd = jnp.transpose(split, (0, 2, 1, 3, 4, 5)).reshape(BLOCKS, 3 * chans, 18 * own)
+    taps = jnp.transpose(temporal_taps, (2, 0, 1)).reshape(chans, 3 * BLOCKS)
+    count = copy_count(phase_n, chan_n, BLOCKS)
+    dims = (phase_n, chan_n, phase_rows, own, whole, chunk)
+    vmem = pl.BlockSpec(memory_space=pltpu.VMEM)
+    final, grad, kernels, tap_sums = pl.pallas_call(
+        functools.partial(fused_kernel, dims),
+        out_shape=(
+            jax.ShapeDtypeStruct((chan_n, own, flat), b16),
+            jax.ShapeDtypeStruct((chan_n, own, flat), b16),
+            jax.ShapeDtypeStruct((BLOCKS, phase_n, chunk, 6 * own), b16),
+            jax.ShapeDtypeStruct((chan_n, own, 128), f32),
+        ),
+        in_specs=[vmem] * 5,
+        out_specs=(vmem,) * 4,
+        scratch_shapes=[
+            pltpu.VMEM((chan_n, own, flat), b16),
+            pltpu.VMEM((chan_n, own, flat), b16),
+            pltpu.VMEM((BLOCKS + 1, own, width), b16),
+            pltpu.VMEM((BLOCKS, own, width), b16),
+            pltpu.VMEM((BLOCKS, own, width), b16),
+            pltpu.VMEM((BLOCKS, chans, width), b16),
+            pltpu.VMEM((BLOCKS, stack_rows, width), b16),
+            pltpu.VMEM((BLOCKS, own, width), f32),
+            pltpu.VMEM((BLOCKS, own, width), f32),
+            pltpu.VMEM((18 * own, width), b16),
+            pltpu.VMEM((BLOCKS, chans, width), b16),
+            pltpu.VMEM((chans, width), f32),
+            pltpu.VMEM((BLOCKS, chan_n, own, width), b16),
+            pltpu.VMEM((BLOCKS, own, width), b16),
+            pltpu.VMEM((BLOCKS, own, width), b16),
+            pltpu.VMEM((BLOCKS, own, width), b16),
+            pltpu.VMEM((BLOCKS, chunk * phase_n, 6 * own), b16),
+            pltpu.VMEM((BLOCKS, phase_n, chunk, 6 * own), b16),
+            pltpu.VMEM((own, 128), f32),
+            pltpu.VMEM((phase_n, own, 128), f32),
+            pltpu.VMEM((chan_n, own, flat), b16),
+            pltpu.VMEM((chan_n, own, flat), b16),
+            pltpu.SemaphoreType.DMA((count,)),
+            pltpu.SemaphoreType.DMA((count,)),
+        ],
+        compiler_params=pltpu.CompilerParams(
+            collective_id=0, has_side_effects=True, vmem_limit_bytes=48 * 1024 * 1024
+        ),
+        name="fused_blocks",
+    )(frames.reshape(chans, flat), cotangent.reshape(chans, flat), taps, w_fwd, w_bwd)
+    final = final.reshape(chans, phase_rows, local)
+    grad = grad.reshape(chans, phase_rows, local)
+    kernels = kernels.reshape(BLOCKS, phase_n * chunk, 6 * own)[:, :stack_rows]
+    kernels = kernels.reshape(BLOCKS, 9, chans, 3, 2, own)
+    kernels = jnp.transpose(kernels, (0, 2, 3, 1, 4, 5)).reshape(conv_weights.shape)
+    tap_sums = tap_sums.reshape(chans, 128)[:, : 3 * BLOCKS]
+    tap_sums = jnp.transpose(tap_sums).reshape(temporal_taps.shape)
+    return (final, grad, tap_sums, kernels.astype(f32))
+
+
+def fits(frames):
+    chans, phase_rows, local = frames.shape
+    phase_n, chan_n = lax.axis_size("phase"), lax.axis_size("chan")
+    whole_hops = all(
+        2**block < phase_rows
+        or (2**block % phase_rows == 0 and (2**block // phase_rows) % phase_n != 0)
+        for block in range(BLOCKS)
+    )
+    return (
+        phase_n > 2
+        and chan_n > 1
+        and chans % (16 * chan_n) == 0
+        and local % 128 == 0
+        and SY * SZ == 128
+        and whole_hops
+    )
+
+
+def any_size(frames, temporal_taps, conv_weights, cotangent):
+    body = fused if fits(frames) else per_device
+    return body(frames, temporal_taps, conv_weights, cotangent)
+
+
 def solution(mesh):
     in_specs = (
         P(None, "phase", "chan"),
@@ -192,5 +630,5 @@
         P(None, None, None, None, "chan"),
     )
     return jax.shard_map(
-        per_device, mesh=mesh, in_specs=in_specs, out_specs=out_specs, check_vma=False
+        any_size, mesh=mesh, in_specs=in_specs, out_specs=out_specs, check_vma=False
     )

time: 320 us -> 96.3 us (0.30)
  blocking collectives: 123 us -> 0 us
  Pallas kernels: 0 us -> 82.1 us
  waiting for transfers between devices: 73.4 us -> 0 us
  starting transfers between devices: 62.1 us -> 0 us
  other arithmetic: 23.7 us -> 0 us
  between operations: 15.7 us -> 0.68 us
  matrix products: 14.8 us -> 0 us
  local copies, waits for them, and re-layouts: 6.33 us -> 13.2 us
    pallas_call x0 -> x1, Pallas kernels: none -> 82.1 us  [fused(): pl.pallas_call(functools.partial(fused_kernel, dims), out_shape=(jax.Shap...]
    all_gather x4 -> x0, blocking collectives: 81.9 us -> none  [per_device(): kernel = lax.all_gather(conv_weights[block_num], 'chan', axis=3, tiled=True)]
    ppermute x30 -> x0, starting transfers between devices: 61.7 us -> none  [the longest x8 30.8 us: padded_2(): lax.ppermute(tail, axis, [(i, (i + 1) % count) for i in range(ends)])]
    psum x1 -> x0, waiting for transfers between devices: 57.9 us -> none  [per_device(): grad_kernel = lax.psum(kernel_piece, 'phase').astype(jnp.float32)]
    psum x1 -> x0, blocking collectives: 41 us -> none  [per_device(): grad_taps = lax.psum(jnp.stack(tap_grads), ('phase', 'chan'))]
    dot_general x60 -> x0, matrix products: 14.8 us -> none  [the longest x36 8.25 us: per_device(): jnp.einsum('okgpv,ikgo->ipv', group, kernel[:, first:first + 3], preferre...]
    ppermute x30 -> x0, waiting for transfers between devices: 14.5 us -> none  [the longest x14 14 us: shifted(): return lax.ppermute(block, axis, route)]
    another operation x39 -> x0, other arithmetic: 14.1 us -> none  [the longest x22 10.7 us: offset_stack(): jnp.stack([shifted_cells(rimmed, sign * offset[0], sign * offset[1], sign...]
  transfers between devices with their start and end apart: 35 -> 0, of which waited for: 11 -> 0; matrix products, arithmetic and copies ran while one was open for 10% -> 0% of each run, Pallas kernels for 0% -> 0%
where the time goes in v1:
time: 96.3 us; the launch traced here: 96 us
  Pallas kernels  82.1 us (85%)
  local copies, waits for them, and re-layouts  13.2 us (14%)
    pallas_call x1, Pallas kernels, fused(): pl.pallas_call(functools.partial(fused_kernel, dims), out_shape=(jax.Shap...  82.1 us
    reshape x2, local copies, waits for them, and re-layouts, fused(): split = conv_weights.reshape(BLOCKS, chans, 3, 9, 2, own)  3.45 us
    convert_element_type x2, local copies, waits for them, and re-layouts, fused(): return (final, grad, tap_sums, kernels.astype(f32))  3.32 us

profile of v1, /device:TPU:0, one launch (start us, length us, event | category | flops | bytes accessed | tf_op | source)
XLA Modules:
  0.0 96.0 jit_solution(14399397906529661041)
XLA Ops:
  0.6 0.7 copy.20
  1.3 0.1 copy.23.taps
  1.4 0.8 copy_bitcast_fusion.2
  2.2 1.8 %copy.38 = bf16[4,64,3,9,2,16]{1,2,5,4,3,0:T(4,128)(2,1)S(1)} copy(bf16[4,64,3,9,2,16]{1,5,4,3,2,0:T(8,128)(2,1)} %bitcast.31) | data formatting | bytes 884736 | tf_op jit(solution)/shard_map/reshape | solution.py:538
  4.0 0.7 reshape.52
  4.7 0.3 copy.24.w_bwd
  5.1 1.7 %copy.37 = bf16[4,64,3,9,2,16]{1,3,5,4,2,0:T(8,128)(2,1)S(1)} copy(bf16[4,64,3,9,2,16]{1,5,4,3,2,0:T(8,128)(2,1)} %bitcast.32) | data formatting | bytes 884736 | tf_op jit(solution)/shard_map/reshape | solution.py:538
  6.8 0.8 reshape.51.w_fwd
  7.5 82.1 %fused_blocks.1 = (bf16[4,16,256]{2,1,0:T(8,128)(2,1)S(1)}, bf16[4,16,256]{2,1,0:T(8,128)(2,1)S(1)}, bf16[4,8,80,96]{3,2,1,0:T(8,128)(2,1)S(1)}, f32[4,16,128]{2,1,0:T(8,128)S(1)}) custom-call(bf16[64,256]{1,0:T(8,128)(2,1)S(1)} %get-tuple-element.21.frames, bf16[64,256]{1,0:T(8,128)(2,1)S(1)} %get-tuple-element.20.cotangent, f32[64,12]{1,0:T(8,128)S(1)} %copy.23.taps, ...), custom_call_target="tpu_custom_call" | custom-call | tf_op jit(solution)/shard_map/fused_blocks/pallas_call | solution.py:545
  89.6 0.6 reshape.53
  90.3 0.1 copy.29
  90.3 0.6 copy.28
  91.0 0.6 reshape.54
  91.6 1.0 %copy.30 = bf16[4,576,96]{1,2,0:T(8,128)(2,1)} copy(bf16[4,576,96]{2,1,0:T(8,128)(2,1)S(1)} %slice.9) | data formatting | bytes 884736
  92.6 1.6 %reshape.59 = f32[4,9,64,3,2,16]{2,1,5,4,3,0:T(8,128)S(1)} reshape(bf16[4,576,96]{1,2,0:T(8,128)(2,1)} %copy.30) | data formatting | bytes 1327104 | tf_op jit(solution)/shard_map/convert_element_type | solution.py:593
  94.2 1.7 %copy.27 = f32[4,64,3,9,2,16]{1,5,4,3,2,0:T(8,128)} copy(f32[4,64,3,9,2,16]{1,3,5,4,2,0:T(8,128)S(1)} %bitcast.28) | data formatting | bytes 1769472 | tf_op jit(solution)/shard_map/convert_element_type | solution.py:593
  (3 shorter events, 0.1 us)

commit v2 on v1

--- a/solution.py
+++ b/solution.py
@@ -205,8 +205,7 @@
 
 def copy_count(phase_n, chan_n, blocks):
     return (
-        4 * (chan_n - 1)
-        + blocks * (2 + (chan_n - 1))
+        blocks * (2 + (chan_n - 1))
         + blocks * ((chan_n - 1) + 2 + 2 * (phase_n - 1))
         + (phase_n - 1)
         + (chan_n - 1)
@@ -234,12 +233,16 @@
     frames,
     cotangent,
     taps,
-    w_fwd,
-    w_bwd,
+    weights,
     final_out,
     grad_out,
     gw_out,
     taps_out,
+    w_fwd,
+    w_bwd,
+    behind_v,
+    ahead_v,
+    gw_all,
     fr_x,
     cot_x,
     state,
@@ -264,6 +267,8 @@
     grad_send,
     send_sems,
     recv_sems,
+    move_send,
+    move_recv,
 ):
     phase_n, chan_n, phase_rows, own, whole, chunk = dims
     chans = own * chan_n
@@ -284,16 +289,24 @@
     def rows_of(index):
         return pl.ds(pl.multiple_of(index * own, own), own)
 
+    half = phase_n // 2
+    q = lax.rem(p, 2) * half + lax.div(p, 2)
+
+    def holder(residue):
+        return lax.rem(residue, half) * 2 + lax.div(residue, half)
+
+    def at_residue(hop):
+        return {"phase": holder(lax.rem(q + (hop % phase_n), phase_n)), "chan": z}
+
+    everyone = phase_n * chan_n
     barrier = pltpu.get_barrier_semaphore()
-    for hop in range(1, phase_n):
+    for hop in range(1, everyone):
+        number = lax.rem(p * chan_n + z + hop, everyone)
+        other = {"phase": lax.div(number, chan_n), "chan": lax.rem(number, chan_n)}
         pl.semaphore_signal(
-            barrier, inc=1, device_id=at_phase(hop), device_id_type=pl.DeviceIdType.MESH
-        )
-    for hop in range(1, chan_n):
-        pl.semaphore_signal(
-            barrier, inc=1, device_id=at_chan(hop), device_id_type=pl.DeviceIdType.MESH
-        )
-    pl.semaphore_wait(barrier, phase_n + chan_n - 2)
+            barrier, inc=1, device_id=other, device_id_type=pl.DeviceIdType.MESH
+        )
+    pl.semaphore_wait(barrier, everyone - 1)
 
     lane = lax.broadcasted_iota(jnp.int32, (1, width), 1)
     coord_z = lax.rem(lane, SZ)
@@ -316,85 +329,120 @@
                 rolled = pltpu.roll(array, (-moved) % width, axis=1)
                 yield (rolled * masks[step_y, step_z]).astype(b16)
 
-    def spread_rows(source, target):
-        got = []
-        for hop in range(1, chan_n):
-            there = at_chan(hop)
-            got.append(copies.send(source.at[rows_of(there["chan"])], target.at[z], there))
-        target[z] = source[rows_of(z), :]
+    moves = []
+
+    def working_place(index):
+        phase = phase_rows * p + index
+        return holder(lax.rem(phase, phase_n)), lax.div(phase, phase_n)
+
+    def home_place(index):
+        phase = q + phase_n * index
+        return lax.div(phase, phase_rows), lax.rem(phase, phase_rows)
+
+    def move(group, source, target, place):
+        for index in range(phase_rows):
+            where, slot = place(index)
+            for hop in range(chan_n):
+                chan = lax.rem(z + hop, chan_n)
+                src, dst = source(index, chan), target.at[slot, z]
+                recv_sem = move_recv.at[group, slot * chan_n + z]
+                copy = pltpu.make_async_remote_copy(
+                    src_ref=src,
+                    dst_ref=dst,
+                    send_sem=move_send.at[group, index * chan_n + hop],
+                    recv_sem=recv_sem,
+                    device_id={"phase": where, "chan": chan},
+                    device_id_type=pl.DeviceIdType.MESH,
+                )
+                if hop:
+                    copy.start()
+                    moves.append((copy, None))
+                else:
+                    pl.when(where != p)(copy.start)
+                    pl.when(where == p)(pltpu.make_async_copy(src, dst, recv_sem).start)
+                    moves.append((copy, where))
+
+    def arrived(group, target):
+        for slot in range(phase_rows):
+            for chan in range(chan_n):
+                part = target.at[slot, chan]
+                pltpu.make_async_copy(
+                    part, part, move_recv.at[group, slot * chan_n + chan]
+                ).wait()
+
+    def join_planes(parts):
+        return jnp.concatenate(
+            [parts[u, chan] for u in range(phase_rows) for chan in range(chan_n)], axis=1
+        )
+
+    def send_home(group, array, stage, target):
+        for u in range(phase_rows):
+            for chan in range(chan_n):
+                base = u * whole + chan * local
+                stage[u, chan] = array[:, base : base + local]
+        move(group, lambda index, chan: stage.at[index, chan], target, home_place)
+
+    def turned(array, count):
+        cut_at = (count % phase_rows) * whole
+        if cut_at == 0:
+            return array
+        return jnp.concatenate([array[:, width - cut_at :], array[:, : width - cut_at]], axis=1)
+
+    def start_neighbours(source, back, ahead, reach):
+        if reach % phase_n == 0:
+            return []
+        got = [copies.send(source, back, at_residue(reach))]
+        if (2 * reach) % phase_n:
+            got.append(copies.send(source, ahead, at_residue(-reach)))
         return got
 
-    def join_planes(parts):
-        pieces = []
-        for row in range(phase_rows):
-            for index in range(chan_n):
-                pieces.append(parts[index, :, row * local : (row + 1) * local])
-        return jnp.concatenate(pieces, axis=1)
-
-    def spread_planes(array, stage, target):
-        for index in range(chan_n):
-            stage[index] = jnp.concatenate(
-                [
-                    array[:, row * whole + index * local : row * whole + (index + 1) * local]
-                    for row in range(phase_rows)
-                ],
-                axis=1,
-            )
-        got = []
-        for hop in range(1, chan_n):
-            there = at_chan(hop)
-            got.append(copies.send(stage.at[there["chan"]], target.at[z], there))
-        target[z] = stage[z]
-        return got
-
-    def start_neighbours(source, back, ahead, reach):
-        hops, rest = divmod(reach, phase_rows)
-        if rest:
-            edge = rest * whole
-            got = [
-                copies.send(source.at[:, width - edge :], back.at[:, :edge], at_phase(1)),
-                copies.send(source.at[:, :edge], ahead.at[:, width - edge :], at_phase(-1)),
-            ]
-            back[:, edge:] = source[:, : width - edge]
-            ahead[:, : width - edge] = source[:, edge:]
-            return got
-        if (2 * hops) % phase_n == 0:
-            return [copies.send(source, back, at_phase(hops))]
-        return [
-            copies.send(source, back, at_phase(hops)),
-            copies.send(source, ahead, at_phase(-hops)),
-        ]
-
-    def read_neighbours(back, ahead, got):
+    def read_neighbours(source, back, ahead, got, reach):
+        if not got:
+            here = source[...].astype(f32)
+            return turned(here, reach // phase_n), turned(here, -(reach // phase_n))
         for copy in got:
             copy.wait_recv()
-        back_values = back[...].astype(f32)
-        if len(got) == 1:
-            return back_values, back_values
-        return back_values, ahead[...].astype(f32)
+        back_raw = back[...].astype(f32)
+        ahead_raw = back_raw if len(got) == 1 else ahead[...].astype(f32)
+        return (
+            jnp.where(q >= reach, back_raw, turned(back_raw, 1)),
+            jnp.where(q + reach < phase_n, ahead_raw, turned(ahead_raw, -1)),
+        )
 
     def wait_all(got):
         for copy in got:
             copy.wait_recv()
 
-    got_frames = spread_rows(frames, fr_x)
-    got_cotangent = spread_rows(cotangent, cot_x)
+    move(0, lambda index, chan: frames.at[index, rows_of(chan), :], fr_x, working_place)
+    move(1, lambda index, chan: cotangent.at[index, rows_of(chan), :], cot_x, working_place)
+    pair = 2 * own
+    for block in range(BLOCKS):
+        for step in range(3):
+            rows = weights[block, step * 9 * pair : (step + 1) * 9 * pair, :]
+            w_fwd[block, step * pair : (step + 1) * pair, :] = jnp.concatenate(
+                [rows[k * pair : (k + 1) * pair] for k in range(9)], axis=1
+            )
+            w_bwd[block, step * chans : (step + 1) * chans, :] = jnp.transpose(
+                rows.astype(f32)
+            ).astype(b16)
     own_taps = taps[rows_of(z), :]
 
     def tap(block, index):
         number = 3 * block + index
         return own_taps[:, number : number + 1]
 
-    wait_all(got_frames)
+    arrived(0, fr_x)
     state[0] = join_planes(fr_x)
 
-    single = []
     for block in range(BLOCKS):
         reach = 2**block
         got = start_neighbours(state.at[block], behind_b.at[block], ahead_b.at[block], reach)
-        single.append(len(got) == 1)
         here = state[block].astype(f32)
-        back, ahead = read_neighbours(behind_b.at[block], ahead_b.at[block], got)
+        back, ahead = read_neighbours(
+            state.at[block], behind_b.at[block], ahead_b.at[block], got, reach
+        )
+        behind_v[block] = back.astype(b16)
+        ahead_v[block] = ahead.astype(b16)
         mix = tap(block, 0) * back + tap(block, 1) * here + tap(block, 2) * ahead
         mixed[block, rows_of(z), :] = mix.astype(b16)
         got = []
@@ -417,9 +465,9 @@
         gate[block] = sig
         state[block + 1] = (here + conv[:own] * sig).astype(b16)
 
-    got_final = spread_planes(state[BLOCKS], final_send, final_out)
-
-    wait_all(got_cotangent)
+    send_home(2, state[BLOCKS], final_send, final_out)
+
+    arrived(1, cot_x)
     grad = join_planes(cot_x).astype(f32)
     tap_lane = lax.broadcasted_iota(jnp.int32, tap_send.shape, 1)
     tap_sums = jnp.zeros(tap_send.shape, f32)
@@ -431,9 +479,9 @@
         for hop in range(1, phase_n):
             source = lax.rem(p + hop, phase_n)
             total = total + gw_recv[block, source].astype(f32)
-        gw_out[block, p] = total.astype(b16)
+        gw_all[block, p] = total.astype(b16)
         for hop in range(1, phase_n):
-            part = gw_out.at[block, p]
+            part = gw_all.at[block, p]
             got_final_grads.append(copies.send(part, part, at_phase(hop)))
 
     def rows_chunk(index):
@@ -467,12 +515,19 @@
             [plane_shift(low, 1, phase_rows), low, plane_shift(low, -1, phase_rows)], axis=0
         )
         products = lax.dot_general(
-            stack[block], sides, (((1,), (1,)), ((), ())), preferred_element_type=f32
-        )
-        gw_send[block, : products.shape[0], :] = products.astype(b16)
-        extra = gw_send.shape[1] - products.shape[0]
-        if extra:
-            gw_send[block, products.shape[0] :, :] = jnp.zeros((extra, products.shape[1]), b16)
+            sides, stack[block], (((1,), (1,)), ((), ())), preferred_element_type=f32
+        ).astype(b16)
+        wide = -(-products.shape[1] // 128) * 128
+        if wide != products.shape[1]:
+            blank = jnp.zeros((6 * own, wide - products.shape[1]), b16)
+            products = jnp.concatenate([products, blank], axis=1)
+        filled = 6 * own * (wide // 128)
+        for tile in range(wide // 128):
+            gw_send[block, tile * 6 * own : (tile + 1) * 6 * own, :] = products[
+                :, tile * 128 : (tile + 1) * 128
+            ]
+        if filled < gw_send.shape[1]:
+            gw_send[block, filled:, :] = jnp.zeros((gw_send.shape[1] - filled, 128), b16)
         kernel_got = []
         for hop in range(1, phase_n):
             there = at_phase(hop)
@@ -487,15 +542,16 @@
             mix_grad = mix_grad + gm_recv[block, lax.rem(z + hop, chan_n)].astype(f32)
         gl[block] = mix_grad.astype(b16)
         got = start_neighbours(gl.at[block], gl_back.at[block], gl_ahead.at[block], reach)
-        ahead_state = behind_b if single[block] else ahead_b
-        for index, factor in enumerate((behind_b, state, ahead_state)):
+        for index, factor in enumerate((behind_v, state, ahead_v)):
             total = jnp.sum(mix_grad * factor[block].astype(f32), axis=1, keepdims=True)
             tap_sums = jnp.where(tap_lane == 3 * block + index, total, tap_sums)
         if waiting is not None:
             reduce_kernel(*waiting)
         waiting = (block, kernel_got)
         low = gl[block].astype(f32)
-        back, ahead = read_neighbours(gl_back.at[block], gl_ahead.at[block], got)
+        back, ahead = read_neighbours(
+            gl.at[block], gl_back.at[block], gl_ahead.at[block], got, reach
+        )
         moved = grad + tap(block, 0) * ahead + tap(block, 1) * low + tap(block, 2) * back
         rounded = moved.astype(b16)
         grad = rounded.astype(f32)
@@ -504,7 +560,7 @@
             tap_got = []
             for hop in range(1, phase_n):
                 tap_got.append(copies.send(tap_send, tap_recv.at[p], at_phase(hop)))
-            got_grad = spread_planes(rounded, grad_send, grad_out)
+            send_home(3, rounded, grad_send, grad_out)
 
     reduce_kernel(*waiting)
     wait_all(tap_got)
@@ -517,10 +573,26 @@
     for hop in range(1, chan_n):
         part = taps_out.at[z]
         got_taps.append(copies.send(part, part, at_chan(hop)))
-    wait_all(got_final)
-    wait_all(got_grad)
+    wait_all(got_final_grads)
+    per_tile = 128 // chans
+    for block in range(BLOCKS):
+        joined = jnp.concatenate([gw_all[block, index] for index in range(phase_n)], axis=0)
+        for step in range(3):
+            for k in range(9):
+                top = (k // per_tile) * 6 * own + step * pair
+                left = (k % per_tile) * chans
+                base = (step * 9 + k) * pair
+                gw_out[block, base : base + pair, :] = joined[
+                    top : top + pair, left : left + chans
+                ]
+    arrived(2, final_out)
+    arrived(3, grad_out)
     wait_all(got_taps)
-    wait_all(got_final_grads)
+    for copy, where in moves:
+        if where is None:
+            copy.wait_send()
+        else:
+            pl.when(where != p)(copy.wait_send)
     for copy in copies.started:
         copy.wait_send()
 
@@ -531,13 +603,11 @@
     own = chans // chan_n
     whole = local * chan_n
     width = phase_rows * whole
-    flat = phase_rows * local
     stack_rows = 9 * chans
-    chunk = -(-stack_rows // (16 * phase_n)) * 16
+    kernel_rows = 6 * own * -(-stack_rows // 128)
+    chunk = -(-kernel_rows // (16 * phase_n)) * 16
     b16, f32 = jnp.bfloat16, jnp.float32
-    split = conv_weights.reshape(BLOCKS, chans, 3, 9, 2, own)
-    w_fwd = jnp.transpose(split, (0, 2, 4, 5, 3, 1)).reshape(BLOCKS, 6 * own, 9 * chans)
-    w_bwd = jnp.transpose(split, (0, 2, 1, 3, 4, 5)).reshape(BLOCKS, 3 * chans, 18 * own)
+    weights = jnp.transpose(conv_weights, (0, 2, 3, 4, 1)).reshape(BLOCKS, 54 * own, chans)
     taps = jnp.transpose(temporal_taps, (2, 0, 1)).reshape(chans, 3 * BLOCKS)
     count = copy_count(phase_n, chan_n, BLOCKS)
     dims = (phase_n, chan_n, phase_rows, own, whole, chunk)
@@ -545,16 +615,21 @@
     final, grad, kernels, tap_sums = pl.pallas_call(
         functools.partial(fused_kernel, dims),
         out_shape=(
-            jax.ShapeDtypeStruct((chan_n, own, flat), b16),
-            jax.ShapeDtypeStruct((chan_n, own, flat), b16),
-            jax.ShapeDtypeStruct((BLOCKS, phase_n, chunk, 6 * own), b16),
+            jax.ShapeDtypeStruct((phase_rows, chan_n, own, local), b16),
+            jax.ShapeDtypeStruct((phase_rows, chan_n, own, local), b16),
+            jax.ShapeDtypeStruct((BLOCKS, 54 * own, chans), b16),
             jax.ShapeDtypeStruct((chan_n, own, 128), f32),
         ),
-        in_specs=[vmem] * 5,
+        in_specs=[vmem] * 4,
         out_specs=(vmem,) * 4,
         scratch_shapes=[
-            pltpu.VMEM((chan_n, own, flat), b16),
-            pltpu.VMEM((chan_n, own, flat), b16),
+            pltpu.VMEM((BLOCKS, 6 * own, 9 * chans), b16),
+            pltpu.VMEM((BLOCKS, 3 * chans, 18 * own), b16),
+            pltpu.VMEM((BLOCKS, own, width), b16),
+            pltpu.VMEM((BLOCKS, own, width), b16),
+            pltpu.VMEM((BLOCKS, phase_n, chunk, 128), b16),
+            pltpu.VMEM((phase_rows, chan_n, own, local), b16),
+            pltpu.VMEM((phase_rows, chan_n, own, local), b16),
             pltpu.VMEM((BLOCKS + 1, own, width), b16),
             pltpu.VMEM((BLOCKS, own, width), b16),
             pltpu.VMEM((BLOCKS, own, width), b16),
@@ -569,25 +644,25 @@
             pltpu.VMEM((BLOCKS, own, width), b16),
             pltpu.VMEM((BLOCKS, own, width), b16),
             pltpu.VMEM((BLOCKS, own, width), b16),
-            pltpu.VMEM((BLOCKS, chunk * phase_n, 6 * own), b16),
-            pltpu.VMEM((BLOCKS, phase_n, chunk, 6 * own), b16),
+            pltpu.VMEM((BLOCKS, chunk * phase_n, 128), b16),
+            pltpu.VMEM((BLOCKS, phase_n, chunk, 128), b16),
             pltpu.VMEM((own, 128), f32),
             pltpu.VMEM((phase_n, own, 128), f32),
-            pltpu.VMEM((chan_n, own, flat), b16),
-            pltpu.VMEM((chan_n, own, flat), b16),
+            pltpu.VMEM((phase_rows, chan_n, own, local), b16),
+            pltpu.VMEM((phase_rows, chan_n, own, local), b16),
             pltpu.SemaphoreType.DMA((count,)),
             pltpu.SemaphoreType.DMA((count,)),
+            pltpu.SemaphoreType.DMA((4, phase_rows * chan_n)),
+            pltpu.SemaphoreType.DMA((4, phase_rows * chan_n)),
         ],
         compiler_params=pltpu.CompilerParams(
             collective_id=0, has_side_effects=True, vmem_limit_bytes=48 * 1024 * 1024
         ),
         name="fused_blocks",
-    )(frames.reshape(chans, flat), cotangent.reshape(chans, flat), taps, w_fwd, w_bwd)
-    final = final.reshape(chans, phase_rows, local)
-    grad = grad.reshape(chans, phase_rows, local)
-    kernels = kernels.reshape(BLOCKS, phase_n * chunk, 6 * own)[:, :stack_rows]
-    kernels = kernels.reshape(BLOCKS, 9, chans, 3, 2, own)
-    kernels = jnp.transpose(kernels, (0, 2, 3, 1, 4, 5)).reshape(conv_weights.shape)
+    )(jnp.swapaxes(frames, 0, 1), jnp.swapaxes(cotangent, 0, 1), taps, weights)
+    final = jnp.swapaxes(final.reshape(phase_rows, chans, local), 0, 1)
+    grad = jnp.swapaxes(grad.reshape(phase_rows, chans, local), 0, 1)
+    kernels = jnp.transpose(kernels.reshape(BLOCKS, 27, 2, own, chans), (0, 4, 1, 2, 3))
     tap_sums = tap_sums.reshape(chans, 128)[:, : 3 * BLOCKS]
     tap_sums = jnp.transpose(tap_sums).reshape(temporal_taps.shape)
     return (final, grad, tap_sums, kernels.astype(f32))
@@ -597,12 +672,12 @@
     chans, phase_rows, local = frames.shape
     phase_n, chan_n = lax.axis_size("phase"), lax.axis_size("chan")
     whole_hops = all(
-        2**block < phase_rows
-        or (2**block % phase_rows == 0 and (2**block // phase_rows) % phase_n != 0)
-        for block in range(BLOCKS)
+        2**block < phase_n or 2**block % phase_n == 0 for block in range(BLOCKS)
     )
     return (
-        phase_n > 2
+        phase_n % 2 == 0
+        and phase_n > 2
+        and 128 % chans == 0
         and chan_n > 1
         and chans % (16 * chan_n) == 0
         and local % 128 == 0

time: 96.3 us -> 84.4 us (0.88)
  local copies, waits for them, and re-layouts: 13.2 us -> 4.74 us
  Pallas kernels: 82.1 us -> 77.3 us
  other arithmetic: 0 us -> 1.45 us
    reshape x8 -> x2, local copies, waits for them, and re-layouts: 7.32 us -> 1.3 us  [the longest x1 0.65 us: fused(): final = jnp.swapaxes(final.reshape(phase_rows, chans, local), 0, 1)]
    pallas_call x1, Pallas kernels: 82.1 us -> 77.3 us  [fused(): pl.pallas_call(functools.partial(fused_kernel, dims), out_shape=(jax.Shap...]
    convert_element_type x2 -> x0, local copies, waits for them, and re-layouts: 3.32 us -> none  [fused(): return (final, grad, tap_sums, kernels.astype(f32))]
    convert_element_type x0 -> x1, other arithmetic: none -> 1.45 us  [fused(): return (final, grad, tap_sums, kernels.astype(f32))]
where the time goes in v2:
time: 84.4 us; the launch traced here: 84.1 us
  Pallas kernels  77.3 us (92%)
  local copies, waits for them, and re-layouts  4.74 us (6%)
  other arithmetic  1.45 us (2%)
    pallas_call x1, Pallas kernels, fused(): pl.pallas_call(functools.partial(fused_kernel, dims), out_shape=(jax.Shap...  77.3 us
    unnamed x4, local copies, waits for them, and re-layouts  1.84 us

profile of v2, /device:TPU:0, one launch (start us, length us, event | category | flops | bytes accessed | tf_op | source)
XLA Modules:
  0.0 84.1 jit_solution(14748439775807420169)
XLA Ops:
  0.6 0.7 copy.15
  1.3 0.1 copy.16.taps
  1.4 0.8 copy_bitcast_fusion.2
  2.2 0.0 copy-start
  2.2 1.2 %copy-done = bf16[4,64,27,2,16]{1,4,3,2,0:T(8,128)(2,1)S(1)} copy-done((bf16[4,64,27,2,16]{1,4,3,2,0:T(8,128)(2,1)S(1)}, bf16[4,64,27,2,16]{1,4,3,2,0:T(8,128)(2,1)}, u32[]{:S(2)}) %copy-start) | copy-done | bytes 442392
  3.4 77.3 %fused_blocks.1 = (bf16[2,4,16,128]{3,2,1,0:T(8,128)(2,1)S(1)}, bf16[2,4,16,128]{3,2,1,0:T(8,128)(2,1)S(1)}, bf16[4,864,64]{2,1,0:T(8,128)(2,1)S(1)}, f32[4,16,128]{2,1,0:T(8,128)S(1)}) custom-call(bf16[2,64,128]{2,1,0:T(8,128)(2,1)S(1)} %get-tuple-element.17.frames, bf16[2,64,128]{2,1,0:T(8,128)(2,1)S(1)} %get-tuple-element.16.cotangent, ...), custom_call_target="tpu_custom_call" | custom-call | tf_op jit(solution)/shard_map/fused_blocks/pallas_call | solution.py:615
  80.7 0.6 copy.27
  81.3 0.6 copy.26
  82.0 0.1 copy.21
  82.1 0.6 copy.20
  82.7 1.5 %convert_bitcast_fusion = f32[4,64,27,2,16]{1,4,3,2,0:T(8,128)} fusion(bf16[4,27,2,16,64]{4,3,2,1,0:T(8,128)(2,1)S(1)} %bitcast.26), kind=kLoop, calls=%fused_computation | loop fusion | flops 221184 | bytes 1327104 | tf_op jit(solution)/shard_map/convert_element_type | solution.py:668
  (2 shorter events, 0.0 us)
Async XLA Ops:
  2.2 1.2 %copy-start = (bf16[4,64,27,2,16]{1,4,3,2,0:T(8,128)(2,1)S(1)}, bf16[4,64,27,2,16]{1,4,3,2,0:T(8,128)(2,1)}, u32[]{:S(2)}) copy-start(bf16[4,64,27,2,16]{1,4,3,2,0:T(8,128)(2,1)} %param.6) | copy-start | bytes 1327108

commit v3 on v2

--- a/solution.py
+++ b/solution.py
@@ -243,6 +243,11 @@
     behind_v,
     ahead_v,
     gw_all,
+    fr_behind,
+    fr_ahead,
+    home_grad,
+    home_gl,
+    gl_stage,
     fr_x,
     cot_x,
     state,
@@ -331,12 +336,14 @@
 
     moves = []
 
-    def working_place(index):
-        phase = phase_rows * p + index
+    phases = phase_n * phase_rows
+
+    def working_place(index, ahead=0):
+        phase = lax.rem(phase_rows * p + index + (ahead % phases), phases)
         return holder(lax.rem(phase, phase_n)), lax.div(phase, phase_n)
 
-    def home_place(index):
-        phase = q + phase_n * index
+    def home_place(index, ahead=0):
+        phase = lax.rem(q + phase_n * index + (ahead % phases), phases)
         return lax.div(phase, phase_rows), lax.rem(phase, phase_rows)
 
     def move(group, source, target, place):
@@ -413,8 +420,12 @@
         for copy in got:
             copy.wait_recv()
 
-    move(0, lambda index, chan: frames.at[index, rows_of(chan), :], fr_x, working_place)
-    move(1, lambda index, chan: cotangent.at[index, rows_of(chan), :], cot_x, working_place)
+    def own_rows(source):
+        return lambda index, chan: source.at[index, rows_of(chan), :]
+
+    move(0, own_rows(frames), fr_x, working_place)
+    move(4, own_rows(frames), fr_behind, functools.partial(working_place, ahead=1))
+    move(5, own_rows(frames), fr_ahead, functools.partial(working_place, ahead=-1))
     pair = 2 * own
     for block in range(BLOCKS):
         for step in range(3):
@@ -436,11 +447,19 @@
 
     for block in range(BLOCKS):
         reach = 2**block
-        got = start_neighbours(state.at[block], behind_b.at[block], ahead_b.at[block], reach)
         here = state[block].astype(f32)
-        back, ahead = read_neighbours(
-            state.at[block], behind_b.at[block], ahead_b.at[block], got, reach
-        )
+        if block == 0:
+            arrived(4, fr_behind)
+            arrived(5, fr_ahead)
+            back = join_planes(fr_behind).astype(f32)
+            ahead = join_planes(fr_ahead).astype(f32)
+        else:
+            got = start_neighbours(
+                state.at[block], behind_b.at[block], ahead_b.at[block], reach
+            )
+            back, ahead = read_neighbours(
+                state.at[block], behind_b.at[block], ahead_b.at[block], got, reach
+            )
         behind_v[block] = back.astype(b16)
         ahead_v[block] = ahead.astype(b16)
         mix = tap(block, 0) * back + tap(block, 1) * here + tap(block, 2) * ahead
@@ -449,6 +468,8 @@
         for hop in range(1, chan_n):
             part = mixed.at[block, rows_of(z), :]
             got.append(copies.send(part, part, at_chan(hop)))
+        if block == 0:
+            move(1, own_rows(cotangent), cot_x, working_place)
         wait_all(got)
         full = mixed[block].astype(f32)
         for number, moved in enumerate(cell_shifts(full, 1)):
@@ -536,33 +557,64 @@
                     gw_send.at[block, rows_chunk(there["phase"]), :], gw_recv.at[block, p], there
                 )
             )
+        if waiting is not None:
+            reduce_kernel(*waiting)
+        waiting = (block, kernel_got)
         wait_all(got)
         mix_grad = gm_full[rows_of(z), :]
         for hop in range(1, chan_n):
             mix_grad = mix_grad + gm_recv[block, lax.rem(z + hop, chan_n)].astype(f32)
         gl[block] = mix_grad.astype(b16)
-        got = start_neighbours(gl.at[block], gl_back.at[block], gl_ahead.at[block], reach)
+        if block == 0:
+            for u in range(phase_rows):
+                for chan in range(chan_n):
+                    base = u * whole + chan * local
+                    gl_stage[u, chan] = gl[0, :, base : base + local]
+            for turn, ahead in enumerate((0, 1, -1)):
+                move(
+                    6 + turn,
+                    lambda index, chan: gl_stage.at[index, chan],
+                    home_gl.at[turn],
+                    functools.partial(home_place, ahead=ahead),
+                )
+        else:
+            got = start_neighbours(gl.at[block], gl_back.at[block], gl_ahead.at[block], reach)
         for index, factor in enumerate((behind_v, state, ahead_v)):
             total = jnp.sum(mix_grad * factor[block].astype(f32), axis=1, keepdims=True)
             tap_sums = jnp.where(tap_lane == 3 * block + index, total, tap_sums)
-        if waiting is not None:
-            reduce_kernel(*waiting)
-        waiting = (block, kernel_got)
-        low = gl[block].astype(f32)
-        back, ahead = read_neighbours(
-            gl.at[block], gl_back.at[block], gl_ahead.at[block], got, reach
-        )
-        moved = grad + tap(block, 0) * ahead + tap(block, 1) * low + tap(block, 2) * back
-        rounded = moved.astype(b16)
-        grad = rounded.astype(f32)
         if block == 0:
             tap_send[...] = tap_sums
             tap_got = []
             for hop in range(1, phase_n):
                 tap_got.append(copies.send(tap_send, tap_recv.at[p], at_phase(hop)))
-            send_home(3, rounded, grad_send, grad_out)
+            break
+        low = gl[block].astype(f32)
+        back, ahead = read_neighbours(
+            gl.at[block], gl_back.at[block], gl_ahead.at[block], got, reach
+        )
+        moved = grad + tap(block, 0) * ahead + tap(block, 1) * low + tap(block, 2) * back
+        rounded = moved.astype(b16)
+        grad = rounded.astype(f32)
+        if block == 1:
+            send_home(3, rounded, grad_send, home_grad)
+
+    per_tile = 128 // chans
+
+    def give_kernel(block):
+        joined = jnp.concatenate([gw_all[block, index] for index in range(phase_n)], axis=0)
+        for step in range(3):
+            for k in range(9):
+                top = (k // per_tile) * 6 * own + step * pair
+                left = (k % per_tile) * chans
+                base = (step * 9 + k) * pair
+                gw_out[block, base : base + pair, :] = joined[
+                    top : top + pair, left : left + chans
+                ]
 
     reduce_kernel(*waiting)
+    wait_all(got_final_grads[: 2 * (phase_n - 1)])
+    for block in reversed(range(BLOCKS - 2, BLOCKS)):
+        give_kernel(block)
     wait_all(tap_got)
     tap_recv[p] = tap_send[...]
     total = tap_recv[0]
@@ -573,20 +625,23 @@
     for hop in range(1, chan_n):
         part = taps_out.at[z]
         got_taps.append(copies.send(part, part, at_chan(hop)))
-    wait_all(got_final_grads)
-    per_tile = 128 // chans
-    for block in range(BLOCKS):
-        joined = jnp.concatenate([gw_all[block, index] for index in range(phase_n)], axis=0)
-        for step in range(3):
-            for k in range(9):
-                top = (k // per_tile) * 6 * own + step * pair
-                left = (k % per_tile) * chans
-                base = (step * 9 + k) * pair
-                gw_out[block, base : base + pair, :] = joined[
-                    top : top + pair, left : left + chans
-                ]
+    arrived(3, home_grad)
+    for turn in range(3):
+        arrived(6 + turn, home_gl.at[turn])
+    for index in range(chan_n):
+        columns = taps[index * own : (index + 1) * own, :]
+        for slot in range(phase_rows):
+            moved = (
+                home_grad[slot, index].astype(f32)
+                + columns[:, 0:1] * home_gl[2, slot, index].astype(f32)
+                + columns[:, 1:2] * home_gl[0, slot, index].astype(f32)
+                + columns[:, 2:3] * home_gl[1, slot, index].astype(f32)
+            )
+            grad_out[slot, index] = moved.astype(b16)
+    wait_all(got_final_grads[2 * (phase_n - 1) :])
+    for block in reversed(range(BLOCKS - 2)):
+        give_kernel(block)
     arrived(2, final_out)
-    arrived(3, grad_out)
     wait_all(got_taps)
     for copy, where in moves:
         if where is None:
@@ -630,6 +685,11 @@
             pltpu.VMEM((BLOCKS, phase_n, chunk, 128), b16),
             pltpu.VMEM((phase_rows, chan_n, own, local), b16),
             pltpu.VMEM((phase_rows, chan_n, own, local), b16),
+            pltpu.VMEM((phase_rows, chan_n, own, local), b16),
+            pltpu.VMEM((3, phase_rows, chan_n, own, local), b16),
+            pltpu.VMEM((phase_rows, chan_n, own, local), b16),
+            pltpu.VMEM((phase_rows, chan_n, own, local), b16),
+            pltpu.VMEM((phase_rows, chan_n, own, local), b16),
             pltpu.VMEM((BLOCKS + 1, own, width), b16),
             pltpu.VMEM((BLOCKS, own, width), b16),
             pltpu.VMEM((BLOCKS, own, width), b16),
@@ -652,8 +712,8 @@
             pltpu.VMEM((phase_rows, chan_n, own, local), b16),
             pltpu.SemaphoreType.DMA((count,)),
             pltpu.SemaphoreType.DMA((count,)),
-            pltpu.SemaphoreType.DMA((4, phase_rows * chan_n)),
-            pltpu.SemaphoreType.DMA((4, phase_rows * chan_n)),
+            pltpu.SemaphoreType.DMA((9, phase_rows * chan_n)),
+            pltpu.SemaphoreType.DMA((9, phase_rows * chan_n)),
         ],
         compiler_params=pltpu.CompilerParams(
             collective_id=0, has_side_effects=True, vmem_limit_bytes=48 * 1024 * 1024

time: 84.4 us -> 79.1 us (0.937)
  Pallas kernels: 77.3 us -> 72 us
    pallas_call x1, Pallas kernels: 77.3 us -> 72 us  [fused(): pl.pallas_call(functools.partial(fused_kernel, dims), out_shape=(jax.Shap...]
where the time goes in v3:
time: 79.1 us; the launch traced here: 78.8 us
  Pallas kernels  72 us (91%)
  local copies, waits for them, and re-layouts  4.74 us (6%)
  other arithmetic  1.45 us (2%)
    pallas_call x1, Pallas kernels, fused(): pl.pallas_call(functools.partial(fused_kernel, dims), out_shape=(jax.Shap...  72 us
    unnamed x4, local copies, waits for them, and re-layouts  1.84 us

profile of v3, /device:TPU:0, one launch (start us, length us, event | category | flops | bytes accessed | tf_op | source)
XLA Modules:
  0.0 78.8 jit_solution(4548381325824889313)
XLA Ops:
  0.6 0.7 copy.15
  1.3 0.1 copy.16.taps
  1.4 0.8 copy_bitcast_fusion.2
  2.2 0.0 copy-start
  2.2 1.2 %copy-done = bf16[4,64,27,2,16]{1,4,3,2,0:T(8,128)(2,1)S(1)} copy-done((bf16[4,64,27,2,16]{1,4,3,2,0:T(8,128)(2,1)S(1)}, bf16[4,64,27,2,16]{1,4,3,2,0:T(8,128)(2,1)}, u32[]{:S(2)}) %copy-start) | copy-done | bytes 442392
  3.4 72.0 %fused_blocks.1 = (bf16[2,4,16,128]{3,2,1,0:T(8,128)(2,1)S(1)}, bf16[2,4,16,128]{3,2,1,0:T(8,128)(2,1)S(1)}, bf16[4,864,64]{2,1,0:T(8,128)(2,1)S(1)}, f32[4,16,128]{2,1,0:T(8,128)S(1)}) custom-call(bf16[2,64,128]{2,1,0:T(8,128)(2,1)S(1)} %get-tuple-element.17.frames, bf16[2,64,128]{2,1,0:T(8,128)(2,1)S(1)} %get-tuple-element.16.cotangent, ...), custom_call_target="tpu_custom_call" | custom-call | tf_op jit(solution)/shard_map/fused_blocks/pallas_call | solution.py:670
  75.4 0.6 copy.27
  76.0 0.6 copy.26
  76.7 0.1 copy.21
  76.8 0.6 copy.20
  77.4 1.5 %convert_bitcast_fusion = f32[4,64,27,2,16]{1,4,3,2,0:T(8,128)} fusion(bf16[4,27,2,16,64]{4,3,2,1,0:T(8,128)(2,1)S(1)} %bitcast.26), kind=kLoop, calls=%fused_computation | loop fusion | flops 221184 | bytes 1327104 | tf_op jit(solution)/shard_map/convert_element_type | solution.py:728
  (2 shorter events, 0.0 us)
Async XLA Ops:
  2.2 1.2 %copy-start = (bf16[4,64,27,2,16]{1,4,3,2,0:T(8,128)(2,1)S(1)}, bf16[4,64,27,2,16]{1,4,3,2,0:T(8,128)(2,1)}, u32[]{:S(2)}) copy-start(bf16[4,64,27,2,16]{1,4,3,2,0:T(8,128)(2,1)} %param.6) | copy-start | bytes 1327108

commit v4 on v3

--- a/solution.py
+++ b/solution.py
@@ -233,11 +233,12 @@
     frames,
     cotangent,
     taps,
-    weights,
+    weights_far,
     final_out,
     grad_out,
     gw_out,
     taps_out,
+    weights,
     w_fwd,
     w_bwd,
     behind_v,
@@ -274,6 +275,7 @@
     recv_sems,
     move_send,
     move_recv,
+    weight_sems,
 ):
     phase_n, chan_n, phase_rows, own, whole, chunk = dims
     chans = own * chan_n
@@ -293,6 +295,15 @@
 
     def rows_of(index):
         return pl.ds(pl.multiple_of(index * own, own), own)
+
+    weight_copies = []
+    for block in range(BLOCKS):
+        weight_copies.append(
+            pltpu.make_async_copy(
+                weights_far.at[block], weights.at[block], weight_sems.at[block]
+            )
+        )
+        weight_copies[-1].start()
 
     half = phase_n // 2
     q = lax.rem(p, 2) * half + lax.div(p, 2)
@@ -427,15 +438,23 @@
     move(4, own_rows(frames), fr_behind, functools.partial(working_place, ahead=1))
     move(5, own_rows(frames), fr_ahead, functools.partial(working_place, ahead=-1))
     pair = 2 * own
-    for block in range(BLOCKS):
+
+    def ready_forward(block):
+        weight_copies[block].wait()
         for step in range(3):
             rows = weights[block, step * 9 * pair : (step + 1) * 9 * pair, :]
             w_fwd[block, step * pair : (step + 1) * pair, :] = jnp.concatenate(
                 [rows[k * pair : (k + 1) * pair] for k in range(9)], axis=1
             )
+
+    def ready_backward(block):
+        for step in range(3):
+            rows = weights[block, step * 9 * pair : (step + 1) * 9 * pair, :]
             w_bwd[block, step * chans : (step + 1) * chans, :] = jnp.transpose(
                 rows.astype(f32)
             ).astype(b16)
+
+    ready_forward(0)
     own_taps = taps[rows_of(z), :]
 
     def tap(block, index):
@@ -470,6 +489,9 @@
             got.append(copies.send(part, part, at_chan(hop)))
         if block == 0:
             move(1, own_rows(cotangent), cot_x, working_place)
+        ready_backward(block)
+        if block + 1 < BLOCKS:
+            ready_forward(block + 1)
         wait_all(got)
         full = mixed[block].astype(f32)
         for number, moved in enumerate(cell_shifts(full, 1)):
@@ -675,9 +697,10 @@
             jax.ShapeDtypeStruct((BLOCKS, 54 * own, chans), b16),
             jax.ShapeDtypeStruct((chan_n, own, 128), f32),
         ),
-        in_specs=[vmem] * 4,
+        in_specs=[vmem] * 3 + [pl.BlockSpec(memory_space=pltpu.HBM)],
         out_specs=(vmem,) * 4,
         scratch_shapes=[
+            pltpu.VMEM((BLOCKS, 54 * own, chans), b16),
             pltpu.VMEM((BLOCKS, 6 * own, 9 * chans), b16),
             pltpu.VMEM((BLOCKS, 3 * chans, 18 * own), b16),
             pltpu.VMEM((BLOCKS, own, width), b16),
@@ -714,6 +737,7 @@
             pltpu.SemaphoreType.DMA((count,)),
             pltpu.SemaphoreType.DMA((9, phase_rows * chan_n)),
             pltpu.SemaphoreType.DMA((9, phase_rows * chan_n)),
+            pltpu.SemaphoreType.DMA((BLOCKS,)),
         ],
         compiler_params=pltpu.CompilerParams(
             collective_id=0, has_side_effects=True, vmem_limit_bytes=48 * 1024 * 1024

time: 79.1 us -> 80.8 us (1.021)
  Pallas kernels: 72 us -> 73.7 us
    pallas_call x1, Pallas kernels: 72 us -> 73.7 us  [fused(): pl.pallas_call(functools.partial(fused_kernel, dims), out_shape=(jax.Shap...]
where the time goes in v4:
time: 80.8 us; the launch traced here: 80.6 us
  Pallas kernels  73.7 us (91%)
  local copies, waits for them, and re-layouts  4.74 us (6%)
  other arithmetic  1.45 us (2%)
    pallas_call x1, Pallas kernels, fused(): pl.pallas_call(functools.partial(fused_kernel, dims), out_shape=(jax.Shap...  73.7 us
    unnamed x4, local copies, waits for them, and re-layouts  1.84 us

profile of v4, /device:TPU:0, one launch (start us, length us, event | category | flops | bytes accessed | tf_op | source)
XLA Modules:
  0.0 80.6 jit_solution(2955578984510168394)
XLA Ops:
  0.6 0.7 copy.15
  1.3 0.1 copy.16.taps
  1.4 0.8 copy_bitcast_fusion.2
  2.2 0.0 copy-start
  2.2 1.2 %copy-done = bf16[4,64,27,2,16]{1,4,3,2,0:T(8,128)(2,1)S(1)} copy-done((bf16[4,64,27,2,16]{1,4,3,2,0:T(8,128)(2,1)S(1)}, bf16[4,64,27,2,16]{1,4,3,2,0:T(8,128)(2,1)}, u32[]{:S(2)}) %copy-start) | copy-done | bytes 442392
  3.4 73.7 %fused_blocks.1 = (bf16[2,4,16,128]{3,2,1,0:T(8,128)(2,1)S(1)}, bf16[2,4,16,128]{3,2,1,0:T(8,128)(2,1)S(1)}, bf16[4,864,64]{2,1,0:T(8,128)(2,1)S(1)}, f32[4,16,128]{2,1,0:T(8,128)S(1)}) custom-call(bf16[2,64,128]{2,1,0:T(8,128)(2,1)S(1)} %get-tuple-element.17.frames, bf16[2,64,128]{2,1,0:T(8,128)(2,1)S(1)} %get-tuple-element.16.cotangent, ...), custom_call_target="tpu_custom_call" | custom-call | tf_op jit(solution)/shard_map/fused_blocks/pallas_call | solution.py:692
  77.1 0.6 copy.27
  77.8 0.6 copy.26
  78.4 0.1 copy.21
  78.5 0.6 copy.20
  79.1 1.5 %convert_bitcast_fusion = f32[4,64,27,2,16]{1,4,3,2,0:T(8,128)} fusion(bf16[4,27,2,16,64]{4,3,2,1,0:T(8,128)(2,1)S(1)} %bitcast.26), kind=kLoop, calls=%fused_computation | loop fusion | flops 221184 | bytes 1327104 | tf_op jit(solution)/shard_map/convert_element_type | solution.py:752
  (2 shorter events, 0.0 us)
Async XLA Ops:
  2.2 1.2 %copy-start = (bf16[4,64,27,2,16]{1,4,3,2,0:T(8,128)(2,1)S(1)}, bf16[4,64,27,2,16]{1,4,3,2,0:T(8,128)(2,1)}, u32[]{:S(2)}) copy-start(bf16[4,64,27,2,16]{1,4,3,2,0:T(8,128)(2,1)} %param.6) | copy-start | bytes 1327108
